TPU v7x, 128 devices: a whole 4x4x4 slice. The times are simulated.
128 devices in a mesh: frame: 8 (over z_lo, x), space: 16 (over z_hi, y, core).
Axes of the slice: x: 4, y: 4, z: 4 (z_hi: 2, z_lo: 2; z = z_hi * 2 + z_lo), core: 2. Of those that a mesh axis runs over, the one named last changes fastest.
Arguments:
- queries: bfloat16 [2, 8, 1920, 3072], P(None, 'frame', 'space'), may hold values from -15 to 15
- keys: bfloat16 [2, 8, 1920, 3072], P(None, 'frame', 'space'), may hold values from -15 to 15
- values: bfloat16 [2, 8, 1920, 3072], P(None, 'frame', 'space'), may hold values from -6 to 6
- grad_out: bfloat16 [2, 8, 1920, 3072], P(None, 'frame', 'space'), may hold values from -6 to 6
- head_class: int32 [2, 24], replicated, may hold values from 0 to 1, as said below
Outputs:
- grad_queries: bfloat16 [2, 8, 1920, 3072], P(None, 'frame', 'space')
- grad_keys: bfloat16 [2, 8, 1920, 3072], P(None, 'frame', 'space')
- grad_values: bfloat16 [2, 8, 1920, 3072], P(None, 'frame', 'space')
Inputs may be any that keep to these rules, and one draw needn't show every extreme that they name: `head_class`: in every layer exactly 16 heads carry one label and the other 8 heads the other. The common label alternates from layer to layer: the first layer may have either, the next the other one.
All inputs are finite; a program needn't handle non-finite values.
Results may differ from a plain program's by a relative error of at most 0.012.
The roundings to bfloat16 on the way count: a program that leaves them out, or rounds other values in their place, can miss the bound.
Values may be sent and summed in bfloat16 or wider, within the bound.
No kernel may reach another device: no remote copies, remote signals or barrier semaphores. Data moves between devices by JAX's collectives and lax.ppermute only.
A program may use at most 128 MiB of HBM per device.

v0:
```python
import math

import jax
import jax.numpy as jnp
from jax import lax
from jax.sharding import PartitionSpec as P

RT = 16
RS = 56
SLOTS = 16
PW = 80


THETA = 256.0


def angle_table(frame_ids, position_ids):
    head_width = RT + 2 * RS
    channel = jnp.arange(head_width, dtype=jnp.int32)
    pair_index = channel // 2
    time_pairs = RT // 2
    space_pairs = RS // 2
    is_time = pair_index < time_pairs
    is_row = jnp.logical_and(pair_index >= time_pairs, pair_index < time_pairs + space_pairs)
    local_pair = jnp.where(
        is_time,
        pair_index,
        jnp.where(is_row, pair_index - time_pairs, pair_index - time_pairs - space_pairs),
    )
    part_width = jnp.where(is_time, RT, RS)
    frequency = THETA ** (-2.0 * local_pair.astype(jnp.float32) / part_width.astype(jnp.float32))
    time_value = frame_ids.astype(jnp.float32)[:, None, None]
    row_value = (position_ids // PW).astype(jnp.float32)[None, :, None]
    column_value = (position_ids % PW).astype(jnp.float32)[None, :, None]
    coordinate = jnp.where(is_time, time_value, jnp.where(is_row, row_value, column_value))
    angles = coordinate * frequency
    return (jnp.cos(angles)[:, :, None, :], jnp.sin(angles)[:, :, None, :])


def partner(values_in):
    upper = jnp.roll(values_in, -1, -1)
    lower = jnp.roll(values_in, 1, -1)
    is_even = jnp.arange(values_in.shape[-1], dtype=jnp.int32) % 2 == 0
    return jnp.where(is_even, -upper, lower)


def rotate(values_in, cosine, sine):
    return values_in * cosine + partner(values_in) * sine


def unrotate(values_in, cosine, sine):
    return values_in * cosine - partner(values_in) * sine


def selections(head_class):
    spatial = (head_class == 0).astype(jnp.int32)
    temporal = 1 - spatial
    slot_ids = jnp.arange(SLOTS, dtype=jnp.int32)[:, None]
    spatial_rank = jnp.cumsum(spatial) - 1
    temporal_rank = jnp.cumsum(temporal) - 1
    spatial_pick = jnp.logical_and(spatial_rank[None, :] == slot_ids, spatial[None, :] == 1)
    temporal_pick = jnp.logical_and(temporal_rank[None, :] == slot_ids, temporal[None, :] == 1)
    return (spatial_pick, temporal_pick)


def attend_rows(queries, key_rows, value_rows, grad_rows):
    row_count, head_width = queries.shape
    scaling = 1.0 / math.sqrt(head_width)
    blocks = 1
    while row_count // blocks > 1280 or row_count % blocks:
        blocks += 1
    block_rows = row_count // blocks

    def advance(totals, pieces):
        key_total, value_total = totals
        query_block, grad_block = pieces
        scores = jnp.dot(query_block, key_rows.T, preferred_element_type=jnp.float32) * scaling
        shifted = jnp.exp(scores - jnp.max(scores, -1, keepdims=True))
        probs = shifted / jnp.sum(shifted, -1, keepdims=True)
        probs_rounded = probs.astype(jnp.bfloat16)
        grad_probs = jnp.dot(grad_block, value_rows.T, preferred_element_type=jnp.float32)
        row_delta = jnp.sum(probs * grad_probs, -1, keepdims=True)
        grad_scores = (scaling * probs * (grad_probs - row_delta)).astype(jnp.bfloat16)
        grad_query = jnp.dot(grad_scores, key_rows, preferred_element_type=jnp.float32).astype(
            jnp.bfloat16
        )
        key_total = key_total + jnp.dot(
            grad_scores.T, query_block, preferred_element_type=jnp.float32
        )
        value_total = value_total + jnp.dot(
            probs_rounded.T, grad_block, preferred_element_type=jnp.float32
        )
        return ((key_total, value_total), grad_query)

    zeros = jnp.zeros((key_rows.shape[0], head_width), jnp.float32)
    (key_total, value_total), grad_query = lax.scan(
        advance,
        (zeros, zeros),
        (
            queries.reshape(blocks, block_rows, head_width),
            grad_rows.reshape(blocks, block_rows, head_width),
        ),
    )
    return (grad_query.reshape(row_count, head_width), key_total, value_total)


def attend_frames(queries, key_rows, value_rows, grad_rows):
    scaling = 1.0 / math.sqrt(queries.shape[-1])
    scores = (
        jnp.einsum("fspe,gspe->spfg", queries, key_rows, preferred_element_type=jnp.float32)
        * scaling
    )
    shifted = jnp.exp(scores - jnp.max(scores, -1, keepdims=True))
    probs = shifted / jnp.sum(shifted, -1, keepdims=True)
    probs_rounded = probs.astype(jnp.bfloat16)
    grad_probs = jnp.einsum(
        "fspe,gspe->spfg", grad_rows, value_rows, preferred_element_type=jnp.float32
    )
    row_delta = jnp.sum(probs * grad_probs, -1, keepdims=True)
    grad_scores = (scaling * probs * (grad_probs - row_delta)).astype(jnp.bfloat16)
    grad_values = jnp.einsum(
        "spfg,fspe->gspe", probs_rounded, grad_rows, preferred_element_type=jnp.float32
    ).astype(jnp.bfloat16)
    grad_queries = jnp.einsum(
        "spfg,gspe->fspe", grad_scores, key_rows, preferred_element_type=jnp.float32
    ).astype(jnp.bfloat16)
    grad_keys = jnp.einsum(
        "spfg,fspe->gspe", grad_scores, queries, preferred_element_type=jnp.float32
    ).astype(jnp.bfloat16)
    return (grad_queries, grad_keys, grad_values)


def spatial_send(pieces):
    return (
        lax.all_to_all(pieces[0], "space", split_axis=1, concat_axis=2, tiled=True),
        lax.all_to_all(pieces[1], "space", split_axis=1, concat_axis=2, tiled=True),
        lax.all_to_all(pieces[2], "space", split_axis=1, concat_axis=2, tiled=True),
        lax.all_to_all(pieces[3], "space", split_axis=1, concat_axis=2, tiled=True),
    )


def spatial_whole(pieces):
    received = spatial_send(pieces)
    frame_count, per_device, row_count, head_width = received[0].shape
    flat = tuple(
        (array.reshape(frame_count * per_device, row_count, head_width) for array in received)
    )
    grad_query, key_total, value_total = lax.map(lambda parts: attend_rows(*parts), flat)
    local_shape = (frame_count, per_device, row_count, head_width)
    grad_query = grad_query.reshape(local_shape)
    grad_key = key_total.astype(jnp.bfloat16).reshape(local_shape)
    grad_value = value_total.astype(jnp.bfloat16).reshape(local_shape)
    return (
        lax.all_to_all(grad_query, "space", split_axis=2, concat_axis=1, tiled=True),
        lax.all_to_all(grad_key, "space", split_axis=2, concat_axis=1, tiled=True),
        lax.all_to_all(grad_value, "space", split_axis=2, concat_axis=1, tiled=True),
    )


def temporal_all(pieces):
    received = (
        lax.all_to_all(pieces[0], "frame", split_axis=1, concat_axis=0, tiled=True),
        lax.all_to_all(pieces[1], "frame", split_axis=1, concat_axis=0, tiled=True),
        lax.all_to_all(pieces[2], "frame", split_axis=1, concat_axis=0, tiled=True),
        lax.all_to_all(pieces[3], "frame", split_axis=1, concat_axis=0, tiled=True),
    )
    grads = attend_frames(*received)
    return (
        lax.all_to_all(grads[0], "frame", split_axis=0, concat_axis=1, tiled=True),
        lax.all_to_all(grads[1], "frame", split_axis=0, concat_axis=1, tiled=True),
        lax.all_to_all(grads[2], "frame", split_axis=0, concat_axis=1, tiled=True),
    )


def one_layer(queries, keys, values, grad_out, layer_class):
    frames_dev, positions_dev, model_width = queries.shape
    head_width = RT + 2 * RS
    head_count = model_width // head_width
    heads_shape = (frames_dev, positions_dev, head_count, head_width)
    frame_ids = lax.axis_index("frame") * frames_dev + jnp.arange(frames_dev, dtype=jnp.int32)
    position_ids = lax.axis_index("space") * positions_dev + jnp.arange(
        positions_dev, dtype=jnp.int32
    )
    cosine, sine = angle_table(frame_ids, position_ids)
    rot_queries = rotate(queries.reshape(heads_shape).astype(jnp.float32), cosine, sine).astype(
        jnp.bfloat16
    )
    rot_keys = rotate(keys.reshape(heads_shape).astype(jnp.float32), cosine, sine).astype(
        jnp.bfloat16
    )
    spatial_pick, temporal_pick = selections(layer_class)
    spatial_sel = spatial_pick.astype(jnp.bfloat16)
    temporal_sel = temporal_pick.astype(jnp.bfloat16)

    def gather_slots(array, chooser):
        return jnp.einsum(
            "fphe,sh->fspe", array, chooser, preferred_element_type=jnp.float32
        ).astype(jnp.bfloat16)

    sources = (rot_queries, rot_keys, values.reshape(heads_shape), grad_out.reshape(heads_shape))
    spatial_parts = tuple((gather_slots(array, spatial_sel) for array in sources))
    spatial_grads = spatial_whole(spatial_parts)
    temporal_parts = tuple((gather_slots(array, temporal_sel) for array in sources))
    returned = temporal_all(temporal_parts)

    def place(spatial_term, temporal_term):
        return jnp.einsum(
            "fspe,sh->fphe", spatial_term, spatial_sel, preferred_element_type=jnp.float32
        ) + jnp.einsum(
            "fspe,sh->fphe", temporal_term, temporal_sel, preferred_element_type=jnp.float32
        )

    flat_shape = (frames_dev, positions_dev, model_width)
    grad_queries = (
        unrotate(place(spatial_grads[0], returned[0]), cosine, sine)
        .astype(jnp.bfloat16)
        .reshape(flat_shape)
    )
    grad_keys = (
        unrotate(place(spatial_grads[1], returned[1]), cosine, sine)
        .astype(jnp.bfloat16)
        .reshape(flat_shape)
    )
    grad_values = place(spatial_grads[2], returned[2]).astype(jnp.bfloat16).reshape(flat_shape)
    return (grad_queries, grad_keys, grad_values)


def on_device(queries, keys, values, grad_out, head_class):
    results = [
        one_layer(
            queries[layer_index],
            keys[layer_index],
            values[layer_index],
            grad_out[layer_index],
            head_class[layer_index],
        )
        for layer_index in range(queries.shape[0])
    ]
    grad_queries = jnp.stack([result[0] for result in results])
    grad_keys = jnp.stack([result[1] for result in results])
    grad_values = jnp.stack([result[2] for result in results])
    return (grad_queries, grad_keys, grad_values)


def solution(mesh):
    placed = (
        P(None, "frame", "space", None),
        P(None, "frame", "space", None),
        P(None, "frame", "space", None),
        P(None, "frame", "space", None),
        P(),
    )
    return jax.shard_map(
        on_device,
        mesh=mesh,
        in_specs=placed,
        out_specs=(
            P(None, "frame", "space", None),
            P(None, "frame", "space", None),
            P(None, "frame", "space", None),
        ),
        check_vma=False,
    )
```

profile of v0, /device:TPU:1, one launch (start us, length us, event | category | flops | bytes accessed | tf_op | source)
XLA Modules:
  0.0 665.7 jit_solution(5293400357733222935)
XLA Ops:
  87.5 8.3 %all-to-all-done.7 = bf16[1,16,120,128]{3,2,0,1:T(8,128)(2,1)} async-done(((bf16[1,16,120,128]{3,2,0,1:T(8,128)(2,1)}), bf16[1,16,120,128]{3,2,0,1:T(8,128)(2,1)}, u32[]{:S(2)}, u32[]{:S(2)}) %all-to-all-start.7) | async-done | bytes 491552 | tf_op jit(solution)/shard_map/all_to_all | solution.py:165
  101.1 8.7 %all-to-all-done.15 = bf16[1,16,120,128]{3,2,0,1:T(8,128)(2,1)} async-done(((bf16[1,16,120,128]{3,2,0,1:T(8,128)(2,1)}), bf16[1,16,120,128]{3,2,0,1:T(8,128)(2,1)}, u32[]{:S(2)}, u32[]{:S(2)}) %all-to-all-start.15) | async-done | bytes 491552 | tf_op jit(solution)/shard_map/all_to_all | solution.py:163
  165.0 8.3 %all-to-all-start.1 = ((bf16[1,16,120,128]{3,2,0,1:T(8,128)(2,1)}), bf16[1,16,120,128]{3,2,0,1:T(8,128)(2,1)S(1)}, u32[]{:S(2)}, u32[]{:S(2)}) async-start(bf16[1,16,120,128]{3,2,0,1:T(8,128)(2,1)} %copy.240), calls=%async_computation.1 | async-start | bytes 983040 | tf_op jit(solution)/shard_map/all_to_all | solution.py:136
  207.7 7.8 %all-to-all-done.2 = bf16[1,16,120,128]{3,2,0,1:T(8,128)(2,1)S(1)} async-done(((bf16[1,16,120,128]{3,2,0,1:T(8,128)(2,1)}), bf16[1,16,120,128]{3,2,0,1:T(8,128)(2,1)S(1)}, u32[]{:S(2)}, u32[]{:S(2)}) %all-to-all-start.2) | async-done | bytes 491552 | tf_op jit(solution)/shard_map/all_to_all | solution.py:138
  238.7 8.7 %all-to-all-done.10 = bf16[1,16,120,128]{3,2,0,1:T(8,128)(2,1)S(1)} async-done(((bf16[1,16,120,128]{3,2,0,1:T(8,128)(2,1)}), bf16[1,16,120,128]{3,2,0,1:T(8,128)(2,1)S(1)}, u32[]{:S(2)}, u32[]{:S(2)}) %all-to-all-start.10) | async-done | bytes 491552 | tf_op jit(solution)/shard_map/all_to_all | solution.py:135
  268.5 41.1 %while.52 = (s32[]{:T(128)}, f32[1920,128]{1,0:T(8,128)S(1)}, f32[1920,128]{1,0:T(8,128)}, bf16[2,960,128]{2,1,0:T(8,128)(2,1)S(1)}, bf16[2,960,128]{2,1,0:T(8,1...) while((s32[]{:T(128)}, f32[1920,128]{1,0:T(8,128)S(1)}, ...), condition=%wide.region_5.6_spmd.clone, body=%wide.region_1.5_spmd.clone.sunk | while | flops 2399106304 | bytes 128330184 | solution.py:96
  309.7 7.8 %all-to-all-start.13 = ((bf16[1,16,120,128]{3,2,0,1:T(8,128)(2,1)}), bf16[1,16,120,128]{3,2,0,1:T(8,128)(2,1)S(1)}, u32[]{:S(2)}, u32[]{:S(2)}) async-start(bf16[1,16,120,128]{3,2,0,1:T(8,128)(2,1)} %copy.274), calls=%async_computation.13 | async-start | bytes 983040 | tf_op jit(solution)/shard_map/all_to_all | solution.py:137
  317.6 7.6 %copy.421 = bf16[1,1,1920,128]{3,1,0,2:T(2,128)(2,1)S(1)} copy(bf16[1,1,1920,128]{3,2,1,0:T(8,128)(2,1)S(1)} %convert_bitcast_fusion.5) | data formatting | bytes 983040 | tf_op jit(solution)/shard_map/reshape | solution.py:152
  325.8 10.8 %reduce.13 = bf16[1920,128]{1,0:T(8,128)(2,1)S(1)} reduce(bf16[1920,1,1,128]{3,2,1,0:T(2,128)(2,1)S(1)} %bitcast.440, bf16[]{:T(256)} %broadcast.628), dimensions={1,2}, to_apply=%bitcast.375.reduce_sub_computation | reduce | bytes 983042
  337.5 7.6 %all-to-all-start.24 = ((bf16[16,2,7680]{2,1,0:T(2,128)(2,1)}), bf16[16,2,7680]{2,1,0:T(2,128)(2,1)}, u32[]{:S(2)}, u32[]{:S(2)}) async-start(bf16[16,2,7680]{2,1,0:T(2,128)(2,1)} %reshape.1148), calls=%async_computation.24 | async-start | bytes 983040 | tf_op jit(solution)/shard_map/all_to_all | solution.py:156
  345.2 40.1 %while.53 = (s32[]{:T(128)}, f32[1920,128]{1,0:T(8,128)S(1)}, f32[1920,128]{1,0:T(8,128)}, bf16[2,960,128]{2,1,0:T(8,128)(2,1)S(1)}, bf16[2,960,128]{2,1,0:T(8,1...) while((s32[]{:T(128)}, f32[1920,128]{1,0:T(8,128)S(1)}, ...), condition=%wide.region_15.16_spmd.clone, body=%wide.region_11.15_spmd.clone.sunk | while | flops 2399106304 | bytes 140126784 | solution.py:96
  386.5 8.0 %copy.420 = bf16[1,1,1920,128]{3,1,0,2:T(2,128)(2,1)S(1)} copy(bf16[1,1,1920,128]{3,2,1,0:T(8,128)(2,1)S(1)} %convert_bitcast_fusion.4) | data formatting | bytes 983040 | tf_op jit(solution)/shard_map/reshape | solution.py:152
  394.6 10.8 %reduce.12 = bf16[1920,128]{1,0:T(8,128)(2,1)S(1)} reduce(bf16[1920,1,1,128]{3,2,1,0:T(2,128)(2,1)S(1)} %bitcast.442, bf16[]{:T(256)} %broadcast.628), dimensions={1,2}, to_apply=%bitcast.374.reduce_sub_computation | reduce | bytes 983042
  413.8 7.6 %copy.422 = bf16[1,1,1920,128]{3,1,0,2:T(2,128)(2,1)S(1)} copy(bf16[1,1,1920,128]{3,2,1,0:T(8,128)(2,1)S(1)} %convert_bitcast_fusion.6) | data formatting | bytes 983040 | tf_op jit(solution)/shard_map/reshape | solution.py:151
  421.5 10.8 %reduce.10 = bf16[1920,128]{1,0:T(8,128)(2,1)S(1)} reduce(bf16[1920,1,1,128]{3,2,1,0:T(2,128)(2,1)S(1)} %bitcast.443, bf16[]{:T(256)} %broadcast.628), dimensions={1,2}, to_apply=%bitcast.376.reduce_sub_computation | reduce | bytes 983042
  440.8 7.6 %copy.424 = bf16[1,1,1920,128]{3,1,0,2:T(2,128)(2,1)S(1)} copy(bf16[1,1,1920,128]{3,2,1,0:T(8,128)(2,1)S(1)} %bitcast.458) | data formatting | bytes 983040 | tf_op jit(solution)/shard_map/reshape | solution.py:150
  448.5 10.8 %reduce.9 = bf16[1920,128]{1,0:T(8,128)(2,1)S(1)} reduce(bf16[1920,1,1,128]{3,2,1,0:T(2,128)(2,1)S(1)} %bitcast.444, bf16[]{:T(256)} %broadcast.628), dimensions={1,2}, to_apply=%bitcast.378.reduce_sub_computation | reduce | bytes 983042
  460.1 8.0 %copy.423 = bf16[1,1,1920,128]{3,1,0,2:T(2,128)(2,1)S(1)} copy(bf16[1,1,1920,128]{3,2,1,0:T(8,128)(2,1)S(1)} %convert_bitcast_fusion.7) | data formatting | bytes 983040 | tf_op jit(solution)/shard_map/reshape | solution.py:151
  468.1 10.8 %reduce.8 = bf16[1920,128]{1,0:T(8,128)(2,1)S(1)} reduce(bf16[1920,1,1,128]{3,2,1,0:T(2,128)(2,1)S(1)} %bitcast.445, bf16[]{:T(256)} %broadcast.628), dimensions={1,2}, to_apply=%bitcast.377.reduce_sub_computation | reduce | bytes 983042
  479.9 7.8 %copy.425 = bf16[1,1,1920,128]{3,1,0,2:T(2,128)(2,1)S(1)} copy(bf16[1,1,1920,128]{3,2,1,0:T(8,128)(2,1)S(1)} %bitcast.459) | data formatting | bytes 983040 | tf_op jit(solution)/shard_map/reshape | solution.py:150
  487.6 10.8 %reduce.11 = bf16[1920,128]{1,0:T(8,128)(2,1)S(1)} reduce(bf16[1920,1,1,128]{3,2,1,0:T(2,128)(2,1)S(1)} %bitcast.441, bf16[]{:T(256)} %broadcast.628), dimensions={1,2}, to_apply=%bitcast.379.reduce_sub_computation | reduce | bytes 983042
  517.2 7.6 %all-to-all-start.14 = ((bf16[16,2,7680]{2,1,0:T(2,128)(2,1)}), bf16[16,2,7680]{2,1,0:T(2,128)(2,1)}, u32[]{:S(2)}, u32[]{:S(2)}) async-start(bf16[16,2,7680]{2,1,0:T(2,128)(2,1)} %reshape.1138), calls=%async_computation.14 | async-start | bytes 983040 | tf_op jit(solution)/shard_map/all_to_all | solution.py:154
  527.2 8.4 %all-to-all-done.14 = bf16[16,2,7680]{2,1,0:T(2,128)(2,1)} async-done(((bf16[16,2,7680]{2,1,0:T(2,128)(2,1)}), bf16[16,2,7680]{2,1,0:T(2,128)(2,1)}, u32[]{:S(2)}, u32[]{:S(2)}) %all-to-all-start.14) | async-done | bytes 491552 | tf_op jit(solution)/shard_map/all_to_all | solution.py:154
  640.3 9.6 %fusion.77 = (bf16[1,120,24,128]{3,2,1,0:T(8,128)(2,1)}, bf16[1,120,24,128]{3,2,1,0:T(8,128)(2,1)}, bf16[1,120,24,128]{3,2,1,0:T(8,128)(2,1)}) fusion(f32[1,120,24,1]{3,2,1,0:T(8,128)} %get-tuple-element.240, f32[1,120,24,127]{3,2,1,0:T(8,128)} %get-tuple-element.242, f32[1,120,24,127]{3,2,1,0:T(8,128)} %get-tuple-element.241, ...), kind=kLoop, calls=%fused_computation.103 | loop fusion | flops 8847360 | bytes 15605888 | tf_op jit(solution)/shard_map/convert_element_type | solution.py:221
  (436 shorter events, 468.9 us)
Async XLA Ops:
  49.6 17.7 %all-to-all-start.5 = ((bf16[1,16,120,128]{3,2,0,1:T(8,128)(2,1)}), bf16[1,16,120,128]{3,2,0,1:T(8,128)(2,1)}, u32[]{:S(2)}, u32[]{:S(2)}) async-start(bf16[1,16,120,128]{3,2,0,1:T(8,128)(2,1)} %copy.246), calls=%async_computation.5 | async-start | bytes 983040 | tf_op jit(solution)/shard_map/all_to_all | solution.py:163
  67.4 14.6 %all-to-all-start.6 = ((bf16[1,16,120,128]{3,2,0,1:T(8,128)(2,1)}), bf16[1,16,120,128]{3,2,0,1:T(8,128)(2,1)}, u32[]{:S(2)}, u32[]{:S(2)}) async-start(bf16[1,16,120,128]{3,2,0,1:T(8,128)(2,1)} %copy.247), calls=%async_computation.6 | async-start | bytes 983040 | tf_op jit(solution)/shard_map/all_to_all | solution.py:162
  81.9 13.9 %all-to-all-start.7 = ((bf16[1,16,120,128]{3,2,0,1:T(8,128)(2,1)}), bf16[1,16,120,128]{3,2,0,1:T(8,128)(2,1)}, u32[]{:S(2)}, u32[]{:S(2)}) async-start(bf16[1,16,120,128]{3,2,0,1:T(8,128)(2,1)} %copy.250), calls=%async_computation.7 | async-start | bytes 983040 | tf_op jit(solution)/shard_map/all_to_all | solution.py:165
  95.8 14.0 %all-to-all-start.15 = ((bf16[1,16,120,128]{3,2,0,1:T(8,128)(2,1)}), bf16[1,16,120,128]{3,2,0,1:T(8,128)(2,1)}, u32[]{:S(2)}, u32[]{:S(2)}) async-start(bf16[1,16,120,128]{3,2,0,1:T(8,128)(2,1)} %copy.278), calls=%async_computation.15 | async-start | bytes 983040 | tf_op jit(solution)/shard_map/all_to_all | solution.py:163
  109.8 14.0 %all-to-all-start.16 = ((bf16[1,16,120,128]{3,2,0,1:T(8,128)(2,1)}), bf16[1,16,120,128]{3,2,0,1:T(8,128)(2,1)}, u32[]{:S(2)}, u32[]{:S(2)}) async-start(bf16[1,16,120,128]{3,2,0,1:T(8,128)(2,1)} %copy.279), calls=%async_computation.16 | async-start | bytes 983040 | tf_op jit(solution)/shard_map/all_to_all | solution.py:162
  123.8 13.9 %all-to-all-start.17 = ((bf16[1,16,120,128]{3,2,0,1:T(8,128)(2,1)}), bf16[1,16,120,128]{3,2,0,1:T(8,128)(2,1)}, u32[]{:S(2)}, u32[]{:S(2)}) async-start(bf16[1,16,120,128]{3,2,0,1:T(8,128)(2,1)} %copy.282), calls=%async_computation.17 | async-start | bytes 983040 | tf_op jit(solution)/shard_map/all_to_all | solution.py:165
  137.7 14.0 %all-to-all-start.18 = ((bf16[1,16,120,128]{3,2,0,1:T(8,128)(2,1)}), bf16[1,16,120,128]{3,2,0,1:T(8,128)(2,1)}, u32[]{:S(2)}, u32[]{:S(2)}) async-start(bf16[1,16,120,128]{3,2,0,1:T(8,128)(2,1)} %copy.283), calls=%async_computation.18 | async-start | bytes 983040 | tf_op jit(solution)/shard_map/all_to_all | solution.py:164
  165.0 19.1 %all-to-all-start.1 = ((bf16[1,16,120,128]{3,2,0,1:T(8,128)(2,1)}), bf16[1,16,120,128]{3,2,0,1:T(8,128)(2,1)S(1)}, u32[]{:S(2)}, u32[]{:S(2)}) async-start(bf16[1,16,120,128]{3,2,0,1:T(8,128)(2,1)} %copy.240), calls=%async_computation.1 | async-start | bytes 983040 | tf_op jit(solution)/shard_map/all_to_all | solution.py:136
  184.1 15.9 %all-to-all-start = ((bf16[1,16,120,128]{3,2,0,1:T(8,128)(2,1)}), bf16[1,16,120,128]{3,2,0,1:T(8,128)(2,1)S(1)}, u32[]{:S(2)}, u32[]{:S(2)}) async-start(bf16[1,16,120,128]{3,2,0,1:T(8,128)(2,1)} %copy.233), calls=%async_computation | async-start | bytes 983040 | tf_op jit(solution)/shard_map/all_to_all | solution.py:135
  199.9 15.6 %all-to-all-start.2 = ((bf16[1,16,120,128]{3,2,0,1:T(8,128)(2,1)}), bf16[1,16,120,128]{3,2,0,1:T(8,128)(2,1)S(1)}, u32[]{:S(2)}, u32[]{:S(2)}) async-start(bf16[1,16,120,128]{3,2,0,1:T(8,128)(2,1)} %copy.241), calls=%async_computation.2 | async-start | bytes 983040 | tf_op jit(solution)/shard_map/all_to_all | solution.py:138
  215.5 16.3 %all-to-all-start.3 = ((bf16[1,16,120,128]{3,2,0,1:T(8,128)(2,1)}), bf16[1,16,120,128]{3,2,0,1:T(8,128)(2,1)}, u32[]{:S(2)}, u32[]{:S(2)}) async-start(bf16[1,16,120,128]{3,2,0,1:T(8,128)(2,1)} %copy.242), calls=%async_computation.3 | async-start | bytes 983040 | tf_op jit(solution)/shard_map/all_to_all | solution.py:137
  231.8 15.6 %all-to-all-start.10 = ((bf16[1,16,120,128]{3,2,0,1:T(8,128)(2,1)}), bf16[1,16,120,128]{3,2,0,1:T(8,128)(2,1)S(1)}, u32[]{:S(2)}, u32[]{:S(2)}) async-start(bf16[1,16,120,128]{3,2,0,1:T(8,128)(2,1)} %copy.265), calls=%async_computation.10 | async-start | bytes 983040 | tf_op jit(solution)/shard_map/all_to_all | solution.py:135
  247.3 15.6 %all-to-all-start.11 = ((bf16[1,16,120,128]{3,2,0,1:T(8,128)(2,1)}), bf16[1,16,120,128]{3,2,0,1:T(8,128)(2,1)S(1)}, u32[]{:S(2)}, u32[]{:S(2)}) async-start(bf16[1,16,120,128]{3,2,0,1:T(8,128)(2,1)} %copy.272), calls=%async_computation.11 | async-start | bytes 983040 | tf_op jit(solution)/shard_map/all_to_all | solution.py:136
  262.9 46.8 %all-to-all-start.12 = ((bf16[1,16,120,128]{3,2,0,1:T(8,128)(2,1)}), bf16[1,16,120,128]{3,2,0,1:T(8,128)(2,1)}, u32[]{:S(2)}, u32[]{:S(2)}) async-start(bf16[1,16,120,128]{3,2,0,1:T(8,128)(2,1)} %copy.273), calls=%async_computation.12 | async-start | bytes 983040 | tf_op jit(solution)/shard_map/all_to_all | solution.py:138
  309.7 27.8 %all-to-all-start.13 = ((bf16[1,16,120,128]{3,2,0,1:T(8,128)(2,1)}), bf16[1,16,120,128]{3,2,0,1:T(8,128)(2,1)S(1)}, u32[]{:S(2)}, u32[]{:S(2)}) async-start(bf16[1,16,120,128]{3,2,0,1:T(8,128)(2,1)} %copy.274), calls=%async_computation.13 | async-start | bytes 983040 | tf_op jit(solution)/shard_map/all_to_all | solution.py:137
  337.5 68.8 %all-to-all-start.24 = ((bf16[16,2,7680]{2,1,0:T(2,128)(2,1)}), bf16[16,2,7680]{2,1,0:T(2,128)(2,1)}, u32[]{:S(2)}, u32[]{:S(2)}) async-start(bf16[16,2,7680]{2,1,0:T(2,128)(2,1)} %reshape.1148), calls=%async_computation.24 | async-start | bytes 983040 | tf_op jit(solution)/shard_map/all_to_all | solution.py:156
  406.3 27.0 %all-to-all-start.26 = ((bf16[16,2,7680]{2,1,0:T(2,128)(2,1)}), bf16[16,2,7680]{2,1,0:T(2,128)(2,1)S(1)}, u32[]{:S(2)}, u32[]{:S(2)}) async-start(bf16[16,2,7680]{2,1,0:T(2,128)(2,1)} %reshape.1146), calls=%async_computation.26 | async-start | bytes 983040 | tf_op jit(solution)/shard_map/all_to_all | solution.py:156
  433.2 70.6 %all-to-all-start.22 = ((bf16[16,2,7680]{2,1,0:T(2,128)(2,1)}), bf16[16,2,7680]{2,1,0:T(2,128)(2,1)S(1)}, u32[]{:S(2)}, u32[]{:S(2)}) async-start(bf16[16,2,7680]{2,1,0:T(2,128)(2,1)} %reshape.1142), calls=%async_computation.22 | async-start | bytes 983040 | tf_op jit(solution)/shard_map/all_to_all | solution.py:155
  503.8 13.4 %all-to-all-start.23 = ((bf16[8,2,120,128]{3,2,1,0:T(8,128)(2,1)}), bf16[8,2,120,128]{3,2,1,0:T(8,128)(2,1)S(1)}, u32[]{:S(2)}, u32[]{:S(2)}) async-start(bf16[8,2,120,128]{3,2,1,0:T(8,128)(2,1)} %copy.298), calls=%async_computation.23 | async-start | bytes 983040 | tf_op jit(solution)/shard_map/all_to_all | solution.py:170
  517.2 18.4 %all-to-all-start.14 = ((bf16[16,2,7680]{2,1,0:T(2,128)(2,1)}), bf16[16,2,7680]{2,1,0:T(2,128)(2,1)}, u32[]{:S(2)}, u32[]{:S(2)}) async-start(bf16[16,2,7680]{2,1,0:T(2,128)(2,1)} %reshape.1138), calls=%async_computation.14 | async-start | bytes 983040 | tf_op jit(solution)/shard_map/all_to_all | solution.py:154
  549.0 16.2 %all-to-all-start.20 = ((bf16[16,2,7680]{2,1,0:T(2,128)(2,1)}), bf16[16,2,7680]{2,1,0:T(2,128)(2,1)}, u32[]{:S(2)}, u32[]{:S(2)}) async-start(bf16[16,2,7680]{2,1,0:T(2,128)(2,1)} %reshape.1144), calls=%async_computation.20 | async-start | bytes 983040 | tf_op jit(solution)/shard_map/all_to_all | solution.py:155
  578.4 16.1 %all-to-all-start.4 = ((bf16[16,2,7680]{2,1,0:T(2,128)(2,1)}), bf16[16,2,7680]{2,1,0:T(2,128)(2,1)}, u32[]{:S(2)}, u32[]{:S(2)}) async-start(bf16[16,2,7680]{2,1,0:T(2,128)(2,1)} %reshape.1140), calls=%async_computation.4 | async-start | bytes 983040 | tf_op jit(solution)/shard_map/all_to_all | solution.py:154
  594.5 13.8 %all-to-all-start.9 = ((bf16[8,2,120,128]{3,2,1,0:T(8,128)(2,1)}), bf16[8,2,120,128]{3,2,1,0:T(8,128)(2,1)S(1)}, u32[]{:S(2)}, u32[]{:S(2)}) async-start(bf16[8,2,120,128]{3,2,1,0:T(8,128)(2,1)} %copy.256), calls=%async_computation.9 | async-start | bytes 983040 | tf_op jit(solution)/shard_map/all_to_all | solution.py:169
  608.4 13.8 %all-to-all-start.25 = ((bf16[8,2,120,128]{3,2,1,0:T(8,128)(2,1)}), bf16[8,2,120,128]{3,2,1,0:T(8,128)(2,1)}, u32[]{:S(2)}, u32[]{:S(2)}) async-start(bf16[8,2,120,128]{3,2,1,0:T(8,128)(2,1)} %copy.303), calls=%async_computation.25 | async-start | bytes 983040 | tf_op jit(solution)/shard_map/all_to_all | solution.py:171
  (102 other events, 1375.4 us)
where the time goes:
time: 678 us; the launch traced here: 666 us
  local copies, waits for them, and re-layouts  184 us (27%)
  starting transfers between devices  143 us (21%)
  waiting for transfers between devices  127 us (19%)
  other arithmetic  111 us (16%)
  matrix products  98.3 us (14%)
    unnamed x12, other arithmetic  67.7 us
    unnamed x193, local copies, waits for them, and re-layouts  36.9 us
    slice x16, local copies, waits for them, and re-layouts, partner(): lower = jnp.roll(values_in, 1, -1)  30.3 us
    dot_general x4, matrix products, advance(): jnp.dot(probs_rounded.T, grad_block, preferred_element_type=jnp.float32)  23.1 us
    all_to_all x2, waiting for transfers between devices, spatial_whole(): lax.all_to_all(grad_query, 'space', split_axis=2, concat_axis=1, tiled=True)  15.8 us
    reshape x2, local copies, waits for them, and re-layouts, spatial_whole(): grad_value = value_total.astype(jnp.bfloat16).reshape(local_shape)  15.7 us
    reshape x2, local copies, waits for them, and re-layouts, spatial_whole(): grad_key = key_total.astype(jnp.bfloat16).reshape(local_shape)  15.6 us
    reshape x2, local copies, waits for them, and re-layouts, spatial_whole(): grad_query = grad_query.reshape(local_shape)  15.4 us
  transfers between devices with their start and end apart: 28, of which 22 were waited for; matrix products, arithmetic and copies ran while one was open for 45% of the time, Pallas kernels for 0%

commit v1 on v0

v1 whole, which is shorter than its diff:
```python
import math

import jax
import jax.numpy as jnp
import numpy as np
from jax import lax
from jax.experimental import pallas as pl
from jax.experimental.pallas import tpu as pltpu
from jax.sharding import PartitionSpec as P

RT = 16
RS = 56
PW = 80
THETA = 256.0
W = RT + 2 * RS
HEADS = 24
LAYERS = 2
FRAMES = 8
SPACES = 16
ROWS = 120
POSITIONS = SPACES * ROWS
HALF = 64
BACK = 4 * ROWS + HALF
QB = 512
PADDED = 2048
KB = 480
TP = 24
GROUP = 4
VMEM = 60 * 1024 * 1024
SCALE = 1.0 / math.sqrt(W)
SCALE2 = SCALE * math.log2(math.e)
F32 = jnp.float32
BF16 = jnp.bfloat16


OUT = (LAYERS, 1, ROWS, HEADS * W)


def whole(shape):
    return pl.BlockSpec(shape, lambda i, h, p: (0,) * len(shape))


def tables():
    channel = np.arange(W)
    pair = channel // 2
    tpairs, spairs = RT // 2, RS // 2
    is_time = pair < tpairs
    is_row = (pair >= tpairs) & (pair < tpairs + spairs)
    local = np.where(is_time, pair, np.where(is_row, pair - tpairs, pair - tpairs - spairs))
    width = np.where(is_time, RT, RS)
    freq = THETA ** (-2.0 * local / width)
    sign = np.where(channel % 2 == 0, -1.0, 1.0)
    time = np.arange(FRAMES)[:, None] * freq
    position = np.arange(POSITIONS)[:, None]
    place = np.where(is_row, position // PW, position % PW) * freq
    return (
        np.cos(time).astype(np.float32),
        (np.sin(time) * sign).astype(np.float32),
        np.cos(place).astype(np.float32),
        (np.sin(place) * sign).astype(np.float32),
    )


def lane_ids(shape):
    return lax.broadcasted_iota(jnp.int32, shape, len(shape) - 1)


def swapped(x):
    up = pltpu.roll(x, W - 1, 1)
    low = pltpu.roll(x, 1, 1)
    return jnp.where(lane_ids(x.shape) % 2 == 0, up, low)


def merged(time_row, place_rows):
    return jnp.where(lane_ids(place_rows.shape) < RT, time_row, place_rows)


def rotate(x, cosine, sine):
    return x * cosine + swapped(x) * sine


def unrotate(x, cosine, sine):
    x = x.astype(BF16).astype(F32)
    return x * cosine - swapped(x) * sine


def pick_heads(hc, layers, spatial, ids):
    def look(h, n, layer):
        mine = (hc[layer, h] == 0) == spatial

        @pl.when(mine)
        def _():
            ids[n] = layer * HEADS + h

        return n + mine.astype(jnp.int32)

    found = jnp.int32(0)
    for layer in layers:
        found = lax.fori_loop(0, HEADS, lambda h, n: look(h, n, layer), found)
    return found


def lanes_of(h):
    return pl.ds(pl.multiple_of(h * W, W), W)


def pack_body(hc, place, q, k, v, g, ct, st, cp, sp, out, count, ids, cos_ref, sin_ref):
    layer = pl.program_id(0)

    @pl.when(layer == 0)
    def _():
        count[0] = 0
        frame = place[0]
        cos_ref[...] = merged(ct[pl.ds(frame, 1), :], cp[...])
        sin_ref[...] = merged(st[pl.ds(frame, 1), :], sp[...])

    first = count[0]
    found = pick_heads(hc, [layer], True, ids)
    count[0] = first + found

    def group(n, put):
        cosine, sine = cos_ref[...], sin_ref[...]
        for i in range(GROUP):
            lanes = lanes_of(ids[n * GROUP + i] - layer * HEADS)
            rq = rotate(q[0, 0, :, lanes].astype(F32), cosine, sine).astype(BF16)
            rk = rotate(k[0, 0, :, lanes].astype(F32), cosine, sine).astype(BF16)
            put(first + n * GROUP + i, rq, rk, v[0, 0, :, lanes], g[0, 0, :, lanes])

    def put_own(slot, *parts):
        for a in range(4):
            out[slot, a] = parts[a]

    def put_shared(slot, rq, rk, vv, gg):
        dest = (slot - SPACES) * 2
        out[dest, 4] = rq
        out[dest, 5] = gg
        out[dest + 1, 4] = rk
        out[dest + 1, 5] = vv

    def step(n, carry):
        own = first + n * GROUP < SPACES
        pl.when(own)(lambda: group(n, put_own))
        pl.when(jnp.logical_not(own))(lambda: group(n, put_shared))
        return carry

    lax.fori_loop(0, found // GROUP, step, 0)


SMALL = pl.BlockSpec((FRAMES, W), lambda i, h, p: (0, 0))
LOCAL = pl.BlockSpec((ROWS, W), lambda i, h, p: (p[1], 0))
PACK_COST = pl.CostEstimate(flops=20_000_000, bytes_accessed=9_000_000, transcendentals=0)


def pack_spatial(meta, arrays, tabs):
    shape = (SPACES, 6, ROWS, W)
    part = pl.BlockSpec((1, 1, ROWS, HEADS * W), lambda l, h, p: (l, 0, 0, 0))
    return pl.pallas_call(
        pack_body,
        grid_spec=pltpu.PrefetchScalarGridSpec(
            num_scalar_prefetch=2,
            grid=(LAYERS,),
            in_specs=[part] * 4 + [SMALL, SMALL, LOCAL, LOCAL],
            out_specs=pl.BlockSpec(shape, lambda l, h, p: (0, 0, 0, 0)),
            scratch_shapes=[
                pltpu.SMEM((1,), jnp.int32),
                pltpu.SMEM((HEADS,), jnp.int32),
                pltpu.VMEM((ROWS, W), F32),
                pltpu.VMEM((ROWS, W), F32),
            ],
        ),
        out_shape=jax.ShapeDtypeStruct(shape, BF16),
        compiler_params=pltpu.CompilerParams(vmem_limit_bytes=VMEM),
        cost_estimate=PACK_COST,
        name="pack_spatial",
    )(*meta, *arrays, *tabs)


def peer(place, step, forward):
    frame = place[0]
    x, z = frame % 4, frame // 4
    dx, dz = step // 2, step % 2
    x = (x + (dx if forward else 4 - dx)) % 4
    return (1 - z if dz else z) * 4 + x


def pack_temporal_body(hc, place, q, k, v, g, ct, st, cp, sp, *rest):
    outs, (ids, cos_ref, sin_ref) = rest[:FRAMES], rest[FRAMES:]
    frame = place[0]
    cos_ref[...] = merged(ct[pl.ds(frame, 1), :], cp[...])
    sin_ref[...] = merged(st[pl.ds(frame, 1), :], sp[...])
    pick_heads(hc, range(LAYERS), False, ids)
    for step in range(FRAMES):
        cosine, sine = cos_ref[...], sin_ref[...]
        dest = peer(place, step, True)
        for i in range(3):
            flat_id = ids[dest * 3 + i]
            layer = flat_id // HEADS
            lanes = lanes_of(flat_id - layer * HEADS)
            out = outs[step]
            out[i * 4] = rotate(q[layer, 0, :, lanes].astype(F32), cosine, sine).astype(BF16)
            out[i * 4 + 1] = rotate(k[layer, 0, :, lanes].astype(F32), cosine, sine).astype(BF16)
            out[i * 4 + 2] = v[layer, 0, :, lanes]
            out[i * 4 + 3] = g[layer, 0, :, lanes]


def pack_temporal(meta, arrays, tabs):
    shape = (12, ROWS, W)
    return pl.pallas_call(
        pack_temporal_body,
        grid_spec=pltpu.PrefetchScalarGridSpec(
            num_scalar_prefetch=2,
            grid=(1,),
            in_specs=[whole(OUT)] * 4 + [SMALL, SMALL, LOCAL, LOCAL],
            out_specs=[whole(shape)] * FRAMES,
            scratch_shapes=[
                pltpu.SMEM((HEADS,), jnp.int32),
                pltpu.VMEM((ROWS, W), F32),
                pltpu.VMEM((ROWS, W), F32),
            ],
        ),
        out_shape=[jax.ShapeDtypeStruct(shape, BF16)] * FRAMES,
        compiler_params=pltpu.CompilerParams(vmem_limit_bytes=VMEM),
        cost_estimate=PACK_COST,
        name="pack_temporal",
    )(*meta, *arrays, *tabs)


CHUNKS = POSITIONS // KB
PAIR = KB // ROWS


def attend_body(q, k, v, g, ct, st, cp, sp, store, scratch):
    qs, ks, vs, gs, kt, qt, gt, s_a, s_b, d_a, d_b, dk, dv, dq = scratch

    def rows(j):
        return pl.ds(pl.multiple_of(j * KB, KB), KB)

    def queries(i):
        return pl.ds(pl.multiple_of(i * QB, QB), QB)

    tail = pl.ds(POSITIONS, PADDED - POSITIONS)
    qs[tail, :] = jnp.zeros((PADDED - POSITIONS, W), BF16)
    gs[tail, :] = jnp.zeros((PADDED - POSITIONS, W), BF16)

    def load(j, carry):
        two = pl.ds(j * PAIR, PAIR)
        for ref, read in ((qs, q), (vs, v), (gs, g)):
            ref[rows(j), :] = read(two).astype(F32).reshape(KB, W).astype(BF16)
        key = k(two).astype(F32).reshape(KB, W)
        ks[rows(j), :] = key.astype(BF16)
        kt[j] = key.T.astype(BF16)
        dk[rows(j), :] = jnp.zeros((KB, W), F32)
        dv[rows(j), :] = jnp.zeros((KB, W), F32)
        return carry

    lax.fori_loop(0, CHUNKS, load, 0)

    def turn(i, carry):
        qt[i] = qs[queries(i), :].astype(F32).T.astype(BF16)
        gt[i] = gs[queries(i), :].astype(F32).T.astype(BF16)
        return carry

    lax.fori_loop(0, PADDED // QB, turn, 0)

    def products(i, j, top, refs):
        s_ref, d_ref = refs
        s = jnp.dot(ks[rows(j), :], qt[i], preferred_element_type=F32)
        s_ref[rows(j), :] = s
        d_ref[rows(j), :] = jnp.dot(vs[rows(j), :], gt[i], preferred_element_type=F32)
        return jnp.maximum(top, jnp.max(s, 0, keepdims=True))

    low = jnp.full((1, QB), -jnp.inf, F32)
    zero = jnp.zeros((1, QB), F32)

    def block(i, after_i, top, refs, after_refs):
        s_ref, d_ref = refs

        def sums(j, carry):
            total, delta, after = carry
            p = jnp.exp2((s_ref[rows(j), :] - top) * SCALE2)
            total = total + jnp.sum(p, 0, keepdims=True)
            delta = delta + jnp.sum(p * d_ref[rows(j), :], 0, keepdims=True)
            return total, delta, products(after_i, j, after, after_refs)

        total, delta, after = lax.fori_loop(0, CHUNKS, sums, (zero, zero, low))
        delta = delta / total
        shift = jnp.log2(total)

        def grads(j, dqt):
            p = jnp.exp2((s_ref[rows(j), :] - top) * SCALE2 - shift)
            ds = (p * ((d_ref[rows(j), :] - delta) * SCALE)).astype(BF16)
            dv[rows(j), :] += jnp.dot(
                p.astype(BF16), gs[queries(i), :], preferred_element_type=F32
            )
            dk[rows(j), :] += jnp.dot(ds, qs[queries(i), :], preferred_element_type=F32)
            return dqt + jnp.dot(kt[j], ds, preferred_element_type=F32)

        dqt = lax.fori_loop(0, CHUNKS, grads, jnp.zeros((W, QB), F32))
        dq[queries(i), :] = dqt.T
        return after

    one, two = (s_a, d_a), (s_b, d_b)
    top = lax.fori_loop(0, CHUNKS, lambda j, t: products(0, j, t, one), low)

    def blocks(n, top):
        top = block(2 * n, 2 * n + 1, top, one, two)
        return block(2 * n + 1, jnp.minimum(2 * n + 2, PADDED // QB - 1), top, two, one)

    lax.fori_loop(0, PADDED // QB // 2, blocks, top)

    def finish(b, carry):
        at = pl.ds(pl.multiple_of(b * ROWS, ROWS), ROWS)
        cosine = merged(ct, cp[at, :])
        sine = merged(st, sp[at, :])
        store(b, unrotate(dq[at, :], cosine, sine), unrotate(dk[at, :], cosine, sine), dv[at, :])
        return carry

    lax.fori_loop(0, SPACES, finish, 0)


def attend_scratch():
    return (
        [pltpu.VMEM((PADDED, W), BF16), pltpu.VMEM((POSITIONS, W), BF16)]
        + [pltpu.VMEM((POSITIONS, W), BF16), pltpu.VMEM((PADDED, W), BF16)]
        + [pltpu.VMEM((CHUNKS, W, KB), BF16)]
        + [pltpu.VMEM((PADDED // QB, W, QB), BF16)] * 2
        + [pltpu.VMEM((POSITIONS, QB), F32)] * 4
        + [pltpu.VMEM((POSITIONS, W), F32)] * 2
        + [pltpu.VMEM((PADDED, W), F32)]
    )


def own_body(hc, place, x, kept, given, ct, st, cp, sp, out, *scratch):
    frame = pl.ds(place[0], 1)
    even = place[1] % 2 == 0

    def store(b, *grads):
        rest = jnp.where(even, kept[b].astype(F32), given[b].astype(F32))
        out[b] = jnp.concatenate(list(grads) + [rest], 0).astype(BF16)

    parts = [lambda two, a=a: x[two, a] for a in range(4)]
    attend_body(*parts, ct[frame, :], st[frame, :], cp, sp, store, scratch)


def shared_body(hc, place, mine, other, ct, st, cp, sp, out, give, *scratch):
    frame = pl.ds(place[0], 1)

    def store(b, gq, gk, gv):
        zero = jnp.zeros((2 * HALF - ROWS, W), F32)
        out[b] = jnp.concatenate([gq, gk[:HALF]], 0).astype(BF16)
        give[b] = jnp.concatenate([gv, gk[HALF:], zero], 0).astype(BF16)

    @pl.when(place[1] % 2 == 0)
    def _():
        parts = (
            lambda two: mine[two, 0],
            lambda two: other[two, 0],
            lambda two: other[two, 1],
            lambda two: mine[two, 1],
        )
        attend_body(*parts, ct[frame, :], st[frame, :], cp, sp, store, scratch)


ATTEND_COST = pl.CostEstimate(
    flops=10 * POSITIONS * POSITIONS * W,
    bytes_accessed=6_000_000,
    transcendentals=POSITIONS * POSITIONS,
)


def attend_own(meta, received, kept, given, tabs):
    shape = (SPACES, BACK, W)
    return pl.pallas_call(
        own_body,
        grid_spec=pltpu.PrefetchScalarGridSpec(
            num_scalar_prefetch=2,
            grid=(1,),
            in_specs=[whole((SPACES, 4, ROWS, W)), whole(kept.shape), whole(given.shape)]
            + [whole(t.shape) for t in tabs],
            out_specs=whole(shape),
            scratch_shapes=attend_scratch(),
        ),
        out_shape=jax.ShapeDtypeStruct(shape, BF16),
        compiler_params=pltpu.CompilerParams(vmem_limit_bytes=VMEM),
        cost_estimate=pl.CostEstimate(flops=0, bytes_accessed=6_000_000, transcendentals=0),
        name="attend_own",
    )(*meta, received, kept, given, *tabs)


def attend_shared(meta, mine, other, tabs):
    shape = (SPACES, ROWS + HALF, W)
    return pl.pallas_call(
        shared_body,
        grid_spec=pltpu.PrefetchScalarGridSpec(
            num_scalar_prefetch=2,
            grid=(1,),
            in_specs=[whole(mine.shape), whole(other.shape)] + [whole(t.shape) for t in tabs],
            out_specs=[whole(shape), whole(shape)],
            scratch_shapes=attend_scratch(),
        ),
        out_shape=[jax.ShapeDtypeStruct(shape, BF16)] * 2,
        compiler_params=pltpu.CompilerParams(vmem_limit_bytes=VMEM),
        cost_estimate=ATTEND_COST,
        name="attend_shared",
    )(*meta, mine, other, *tabs)


def frames_body(hc, place, *refs):
    xs, (ct, st, cp, sp) = refs[:FRAMES], refs[FRAMES : FRAMES + 4]
    outs, (dq_ref, dk_ref, dv_ref) = refs[FRAMES + 4 : -3], refs[-3:]
    tokens = FRAMES * TP
    key_place = lax.broadcasted_iota(jnp.int32, (tokens, tokens), 0) % TP
    query_place = lax.broadcasted_iota(jnp.int32, (tokens, tokens), 1) % TP
    same = key_place == query_place
    nt = (((1,), (1,)), ((), ()))
    owners = [peer(place, step, False) for step in range(FRAMES)]

    def head(i, carry):
        for c in range(ROWS // TP):
            rows = slice(c * TP, (c + 1) * TP)
            q, k, v, g = (
                jnp.concatenate([x[i * 4 + a].astype(F32)[rows] for x in xs], 0).astype(BF16)
                for a in range(4)
            )
            s = lax.dot_general(k, q, nt, preferred_element_type=F32)
            s = jnp.where(same, s, -jnp.inf)
            p = jnp.exp2((s - jnp.max(s, 0, keepdims=True)) * SCALE2)
            p = p * (1.0 / jnp.sum(p, 0, keepdims=True))
            d = lax.dot_general(v, g, nt, preferred_element_type=F32)
            delta = jnp.sum(p * d, 0, keepdims=True)
            ds = p * ((d - delta) * SCALE)
            dst = ds.T.astype(BF16)
            ds = ds.astype(BF16)
            gv = jnp.dot(p.astype(BF16), g, preferred_element_type=F32)
            gk = jnp.dot(ds, q, preferred_element_type=F32)
            gq = jnp.dot(dst, k, preferred_element_type=F32)
            place_c, place_s = cp[rows, :], sp[rows, :]
            cosine = jnp.concatenate([merged(ct[pl.ds(f, 1), :], place_c) for f in owners], 0)
            sine = jnp.concatenate([merged(st[pl.ds(f, 1), :], place_s) for f in owners], 0)
            dq_ref[:, rows, :] = unrotate(gq, cosine, sine).reshape(FRAMES, TP, W)
            dk_ref[:, rows, :] = unrotate(gk, cosine, sine).reshape(FRAMES, TP, W)
            dv_ref[:, rows, :] = gv.reshape(FRAMES, TP, W)
        for step, out in enumerate(outs):
            out[i * 3] = dq_ref[step].astype(BF16)
            out[i * 3 + 1] = dk_ref[step].astype(BF16)
            out[i * 3 + 2] = dv_ref[step].astype(BF16)
        return carry

    lax.fori_loop(0, 3, head, 0)


def attend_frames(meta, received, tabs):
    shape = (9, ROWS, W)
    return pl.pallas_call(
        frames_body,
        grid_spec=pltpu.PrefetchScalarGridSpec(
            num_scalar_prefetch=2,
            grid=(1,),
            in_specs=[whole(x.shape) for x in received] + [SMALL, SMALL, LOCAL, LOCAL],
            out_specs=[whole(shape)] * FRAMES,
            scratch_shapes=[pltpu.VMEM((FRAMES, ROWS, W), F32)] * 3,
        ),
        out_shape=[jax.ShapeDtypeStruct(shape, BF16)] * FRAMES,
        compiler_params=pltpu.CompilerParams(vmem_limit_bytes=VMEM),
        cost_estimate=pl.CostEstimate(
            flops=2_000_000_000, bytes_accessed=6_000_000, transcendentals=600_000
        ),
        name="attend_frames",
    )(*meta, *received, *tabs)


def unpack_spatial_body(hc, place, x, oq, ok, ov, count):
    count[0] = 0

    def head(i, carry):
        layer = i // HEADS
        h = i - layer * HEADS

        @pl.when(hc[layer, h] == 0)
        def _():
            slot = count[0]
            count[0] = slot + 1
            lanes = pl.ds(pl.multiple_of(h * W, W), W)

            @pl.when(slot < SPACES)
            def _():
                piece = x[slot].astype(F32)
                oq[layer, 0, :, lanes] = piece[:ROWS].astype(BF16)
                ok[layer, 0, :, lanes] = piece[ROWS : 2 * ROWS].astype(BF16)
                ov[layer, 0, :, lanes] = piece[2 * ROWS : 3 * ROWS].astype(BF16)

            @pl.when(slot >= SPACES)
            def _():
                first = (slot - SPACES) * 2
                one = x[first].astype(F32)
                two = x[first + 1].astype(F32)
                oq[layer, 0, :, lanes] = one[3 * ROWS : 4 * ROWS].astype(BF16)
                ov[layer, 0, :, lanes] = two[3 * ROWS : 4 * ROWS].astype(BF16)
                both = jnp.concatenate([one[4 * ROWS :], two[4 * ROWS : 5 * ROWS - HALF]], 0)
                ok[layer, 0, :, lanes] = both.astype(BF16)

        return carry

    lax.fori_loop(0, LAYERS * HEADS, head, 0)


def unpack_spatial(meta, returned):
    return pl.pallas_call(
        unpack_spatial_body,
        grid_spec=pltpu.PrefetchScalarGridSpec(
            num_scalar_prefetch=2,
            grid=(1,),
            in_specs=[whole(returned.shape)],
            out_specs=[whole(OUT)] * 3,
            scratch_shapes=[pltpu.SMEM((1,), jnp.int32)],
        ),
        out_shape=[jax.ShapeDtypeStruct(OUT, BF16)] * 3,
        compiler_params=pltpu.CompilerParams(vmem_limit_bytes=VMEM),
        cost_estimate=pl.CostEstimate(flops=5_000_000, bytes_accessed=7_000_000, transcendentals=0),
        name="unpack_spatial",
    )(*meta, returned)


def unpack_temporal_body(hc, place, *refs):
    xs, outs, (ids, sems) = refs[:FRAMES], refs[FRAMES + 3 : FRAMES + 6], refs[FRAMES + 6 :]
    pick_heads(hc, range(LAYERS), False, ids)
    copies = []
    for step in range(FRAMES):
        dest = peer(place, step, True)
        for i in range(3):
            flat_id = ids[dest * 3 + i]
            layer = flat_id // HEADS
            lanes = lanes_of(flat_id - layer * HEADS)
            for a in range(3):
                copies.append(
                    pltpu.make_async_copy(
                        xs[step].at[i * 3 + a],
                        outs[a].at[layer, 0, :, lanes],
                        sems.at[step * 3 + i, a],
                    )
                )
                copies[-1].start()
    for copy in copies:
        copy.wait()


def unpack_temporal(meta, returned, partial):
    anywhere = pl.BlockSpec(memory_space=pl.ANY)
    return pl.pallas_call(
        unpack_temporal_body,
        grid_spec=pltpu.PrefetchScalarGridSpec(
            num_scalar_prefetch=2,
            grid=(1,),
            in_specs=[whole(x.shape) for x in returned] + [anywhere] * 3,
            out_specs=[anywhere] * 3,
            scratch_shapes=[
                pltpu.SMEM((HEADS,), jnp.int32),
                pltpu.SemaphoreType.DMA((HEADS, 3)),
            ],
        ),
        out_shape=[jax.ShapeDtypeStruct(OUT, BF16)] * 3,
        input_output_aliases={2 + FRAMES + a: a for a in range(3)},
        compiler_params=pltpu.CompilerParams(vmem_limit_bytes=VMEM),
        cost_estimate=pl.CostEstimate(flops=0, bytes_accessed=5_000_000, transcendentals=0),
        name="unpack_temporal",
    )(*meta, *returned, *partial)


def exchange(x):
    return lax.all_to_all(x, "space", split_axis=0, concat_axis=0, tiled=True)


SWAP = [(i, i ^ 1) for i in range(SPACES)]


def along_x(parts, sign):
    def move(step, part):
        dx = sign * (step // 2)
        if dx == 0:
            return part
        pairs = [(f, f // 4 * 4 + (f + dx) % 4) for f in range(FRAMES)]
        return lax.ppermute(part, "frame", pairs)

    return [move(step, part) for step, part in enumerate(parts)]


def along_z(parts):
    pairs = [(f, f ^ 4) for f in range(FRAMES)]
    return [lax.ppermute(x, "frame", pairs) if n % 2 else x for n, x in enumerate(parts)]


def on_device(queries, keys, values, grad_out, head_class):
    place = jnp.stack([lax.axis_index("frame"), lax.axis_index("space")]).astype(jnp.int32)
    meta = (head_class, place)
    tabs = tuple(jnp.asarray(t) for t in tables())
    arrays = (queries, keys, values, grad_out)
    got_s = exchange(pack_spatial(meta, arrays, tabs))
    half_t = along_x(pack_temporal(meta, arrays, tabs), 1)
    got_s, *half_t = lax.optimization_barrier((got_s, *half_t))
    got_t = along_z(half_t)
    mine = got_s[:, 4:6]
    other = lax.ppermute(mine, "space", SWAP)
    kept, give = attend_shared(meta, mine, other, tabs)
    given = lax.ppermute(give, "space", SWAP)
    back_s = attend_own(meta, got_s, kept, given, tabs)
    back_s, *got_t = lax.optimization_barrier((back_s, *got_t))
    home_s = exchange(back_s)
    home_t = along_z(along_x(attend_frames(meta, got_t, tabs), -1))
    partial = unpack_spatial(meta, home_s)
    return tuple(unpack_temporal(meta, home_t, partial))


def solution(mesh):
    placed = P(None, "frame", "space", None)
    return jax.shard_map(
        on_device,
        mesh=mesh,
        in_specs=(placed, placed, placed, placed, P()),
        out_specs=(placed, placed, placed),
        check_vma=False,
    )
```

time: 678 us -> 195 us (0.29); the launches traced: 666 us -> 194 us
  local copies, waits for them, and re-layouts: 184 us -> 5.64 us
  other arithmetic: 111 us -> 0.61 us
  matrix products: 98.3 us -> 0 us
  starting transfers between devices: 143 us -> 62 us
  waiting for transfers between devices: 127 us -> 59.1 us
  Pallas kernels: 0 us -> 65.5 us
    all_to_all x28 -> x2, waiting for transfers between devices: 127 us -> 0.01 us  [exchange(): return lax.all_to_all(x, 'space', split_axis=0, concat_axis=0, tiled=True)]
    all_to_all x28 -> x2, starting transfers between devices: 143 us -> 17 us  [exchange(): return lax.all_to_all(x, 'space', split_axis=0, concat_axis=0, tiled=True)]
    dot_general x56 -> x0, matrix products: 94.3 us -> none  [the longest x4 23.1 us: advance(): jnp.dot(probs_rounded.T, grad_block, preferred_element_type=jnp.float32)]
    unnamed x12 -> x0, other arithmetic: 67.7 us -> none
    pallas_call x0 -> x7, Pallas kernels: none -> 65.5 us  [the longest x1 28 us: attend_own(): pl.pallas_call(own_body, grid_spec=pltpu.PrefetchScalarGridSpec(num_scala...]
    ppermute x0 -> x22, waiting for transfers between devices: none -> 59.1 us  [the longest x12 32 us: move(): return lax.ppermute(part, 'frame', pairs)]
    reshape x6 -> x0, local copies, waits for them, and re-layouts: 46.7 us -> none  [the longest x2 15.7 us: spatial_whole(): grad_value = value_total.astype(jnp.bfloat16).reshape(local_shape)]
    ppermute x0 -> x22, starting transfers between devices: none -> 44.9 us  [the longest x1 23.7 us: on_device(): given = lax.ppermute(give, 'space', SWAP)]
  transfers between devices with their start and end apart: 28 -> 24, of which waited for: 22 -> 9; matrix products, arithmetic and copies ran while one was open for 45% -> 0% of each run, Pallas kernels for 0% -> 26%
where the time goes in v1:
time: 195 us; the launch traced here: 194 us
  Pallas kernels  65.5 us (34%)
  starting transfers between devices  62 us (32%)
  waiting for transfers between devices  59.1 us (30%)
  local copies, waits for them, and re-layouts  5.64 us (3%)
    ppermute x12, waiting for transfers between devices, move(): return lax.ppermute(part, 'frame', pairs)  32 us
    pallas_call x1, Pallas kernels, attend_own(): pl.pallas_call(own_body, grid_spec=pltpu.PrefetchScalarGridSpec(num_scala...  28 us
    ppermute x8, waiting for transfers between devices, along_z(): lax.ppermute(x, 'frame', pairs)  24.8 us
    ppermute x1, starting transfers between devices, on_device(): given = lax.ppermute(give, 'space', SWAP)  23.7 us
    all_to_all x2, starting transfers between devices, exchange(): return lax.all_to_all(x, 'space', split_axis=0, concat_axis=0, tiled=True)  17 us
    ppermute x12, starting transfers between devices, move(): return lax.ppermute(part, 'frame', pairs)  14.5 us
    pallas_call x1, Pallas kernels, attend_frames(): pl.pallas_call(frames_body, grid_spec=pltpu.PrefetchScalarGridSpec(num_sc...  10 us
    pallas_call x1, Pallas kernels, pack_temporal(): pl.pallas_call(pack_temporal_body, grid_spec=pltpu.PrefetchScalarGridSpec...  6.65 us
  transfers between devices with their start and end apart: 24, of which 9 were waited for; matrix products, arithmetic and copies ran while one was open for 0% of the time, Pallas kernels for 26%

profile of v1, /device:TPU:1, one launch (start us, length us, event | category | flops | bytes accessed | tf_op | source)
XLA Modules:
  0.0 193.7 jit_solution(17482640673379448059)
XLA Ops:
  1.2 6.4 %pack_spatial.1 = bf16[16,6,120,128]{3,2,1,0:T(8,128)(2,1)} custom-call(s32[2,24]{1,0:T(2,128)} %hc.13, s32[2]{0:T(128)} %pad_add_fusion.place, bf16[2,1,120,3072]{3,2,1,0:T(8,128)(2,1)} %q.3, bf16[2,1,120,3072]{3,2,1,0:T(8,128)(2,1)} %k.3, bf16[2,1,120,3072]{3,2,1,0:T(8,128)(2,1)} %v.3, bf16[2,1,120,3072]{3,2,1,0:T(8,128)(2,1)} %g.3, ...), custom_call_target="tpu_custom_call" | custom-call | flops 20000000 | bytes 9000000 | tf_op jit(solution)/shard_map/pack_spatial/pallas_call | solution.py:157
  7.6 9.3 %all-to-all-start = ((bf16[16,6,120,128]{3,2,1,0:T(8,128)(2,1)}), bf16[16,6,120,128]{3,2,1,0:T(8,128)(2,1)S(1)}, u32[]{:S(2)}, u32[]{:S(2)}) async-start(bf16[16,6,120,128]{3,2,1,0:T(8,128)(2,1)} %pack_spatial.1), calls=%async_computation | async-start | bytes 5898240 | tf_op jit(solution)/shard_map/all_to_all | solution.py:570
  16.9 6.7 %pack_temporal.1 = (bf16[12,120,128]{2,1,0:T(8,128)(2,1)}, bf16[12,120,128]{2,1,0:T(8,128)(2,1)}, bf16[12,120,128]{2,1,0:T(8,128)(2,1)}, bf16[12,120,128]{2,1,0:...) custom-call(s32[2,24]{1,0:T(2,128)} %hc.13, ...), custom_call_target="tpu_custom_call" | custom-call | flops 20000000 | bytes 9000000 | tf_op jit(solution)/shard_map/pack_temporal/pallas_call | solution.py:208
  26.0 1.4 collective-permute-start.2
  27.4 1.5 collective-permute-start.3
  29.0 1.5 collective-permute-start.4
  30.5 4.7 %collective-permute-done.refs_2_ = bf16[12,120,128]{2,1,0:T(8,128)(2,1)S(1)} collective-permute-done((bf16[12,120,128]{2,1,0:T(8,128)(2,1)}, bf16[12,120,128]{2,1,0:T(8,128)(2,1)S(1)}, u32[]{:S(2)}, u32[]{:S(2)}) %collective-permute-start) | collective-permute-done | bytes 368672 | tf_op jit(solution)/shard_map/ppermute | solution.py:582
  36.4 6.6 %collective-permute-done.1 = bf16[12,120,128]{2,1,0:T(8,128)(2,1)S(1)} collective-permute-done((bf16[12,120,128]{2,1,0:T(8,128)(2,1)}, bf16[12,120,128]{2,1,0:T(8,128)(2,1)S(1)}, u32[]{:S(2)}, u32[]{:S(2)}) %collective-permute-start.1) | collective-permute-done | bytes 368672 | tf_op jit(solution)/shard_map/ppermute | solution.py:582
  43.0 8.9 %collective-permute-done.2.refs_4_ = bf16[12,120,128]{2,1,0:T(8,128)(2,1)S(1)} collective-permute-done((bf16[12,120,128]{2,1,0:T(8,128)(2,1)}, bf16[12,120,128]{2,1,0:T(8,128)(2,1)S(1)}, u32[]{:S(2)}, u32[]{:S(2)}) %collective-permute-start.2) | collective-permute-done | bytes 368672 | tf_op jit(solution)/shard_map/ppermute | solution.py:582
  51.9 7.9 %collective-permute-done.3 = bf16[12,120,128]{2,1,0:T(8,128)(2,1)S(1)} collective-permute-done((bf16[12,120,128]{2,1,0:T(8,128)(2,1)}, bf16[12,120,128]{2,1,0:T(8,128)(2,1)S(1)}, u32[]{:S(2)}, u32[]{:S(2)}) %collective-permute-start.3) | collective-permute-done | bytes 368672 | tf_op jit(solution)/shard_map/ppermute | solution.py:582
  63.4 2.3 %collective-permute-done.6.other = bf16[16,2,120,128]{3,2,1,0:T(8,128)(2,1)} collective-permute-done((bf16[16,2,120,128]{3,2,1,0:T(8,128)(2,1)S(1)}, bf16[16,2,120,128]{3,2,1,0:T(8,128)(2,1)}, u32[]{:S(2)}, u32[]{:S(2)}) %collective-permute-start.6) | collective-permute-done | bytes 983072 | tf_op jit(solution)/shard_map/ppermute | solution.py:602
  65.7 3.9 %attend_shared.1 = (bf16[16,184,128]{2,1,0:T(8,128)(2,1)}, bf16[16,184,128]{2,1,0:T(8,128)(2,1)}) custom-call(s32[2,24]{1,0:T(2,128)} %hc.13, s32[2]{0:T(128)} %pad_add_fusion.place, bf16[16,2,120,128]{3,2,1,0:T(8,128)(2,1)} %copy-done.2, bf16[16,2,120,128]{3,2,1,0:T(8,128)(2,1)} %collective-permute-done.6.other, f32[8,128]{1,0:T(8,128)} %constant.17.clone.ct.refs_8_, ...), custom_call_target="tpu_custom_call" | custom-call | flops 4718592000 | bytes 6000000 | tf_op jit(solution)/shard_map/attend_shared/pallas_call | solution.py:392
  69.6 23.7 %collective-permute-start.7 = (bf16[16,184,128]{2,1,0:T(8,128)(2,1)}, bf16[16,184,128]{2,1,0:T(8,128)(2,1)S(1)}, u32[]{:S(2)}, u32[]{:S(2)}) collective-permute-start(bf16[16,184,128]{2,1,0:T(8,128)(2,1)} %get-tuple-element.52), channel_id=1, source_target_pairs={{0,1},{1,0},{2,3},{3,2},{4,5},{5,4},{6,7},{7,6},{8,9},{9,8},{10,11... | collective-permute-start | bytes 2261000 | tf_op jit(solution)/shard_map/ppermute | solution.py:604
  97.1 28.0 %attend_own.1 = bf16[16,544,128]{2,1,0:T(8,128)(2,1)} custom-call(s32[2,24]{1,0:T(2,128)} %hc.13, s32[2]{0:T(128)} %pad_add_fusion.place, bf16[16,6,120,128]{3,2,1,0:T(8,128)(2,1)} %copy-done, bf16[16,184,128]{2,1,0:T(8,128)(2,1)} %get-tuple-element.51.kept, bf16[16,184,128]{2,1,0:T(8,128)(2,1)} %copy-done.3, f32[8,128]{1,0:T(8,128)} %constant.17.clone.ct.refs_8_, ...), custom_call_target="tpu_custom_call" | custom-call | bytes 6000000 | tf_op jit(solution)/shard_map/attend_own/pallas_call | solution.py:373
  125.2 2.2 %collective-permute-done.11.refs_7_ = bf16[12,120,128]{2,1,0:T(8,128)(2,1)S(1)} collective-permute-done((bf16[12,120,128]{2,1,0:T(8,128)(2,1)}, bf16[12,120,128]{2,1,0:T(8,128)(2,1)S(1)}, u32[]{:S(2)}, u32[]{:S(2)}) %collective-permute-start.11) | collective-permute-done | bytes 368672 | tf_op jit(solution)/shard_map/ppermute | solution.py:589
  128.1 7.7 %all-to-all-start.1 = ((bf16[16,544,128]{2,1,0:T(8,128)(2,1)}), bf16[16,544,128]{2,1,0:T(8,128)(2,1)S(1)}, u32[]{:S(2)}, u32[]{:S(2)}) async-start(bf16[16,544,128]{2,1,0:T(8,128)(2,1)} %attend_own.1), calls=%async_computation.1 | async-start | bytes 4456448 | tf_op jit(solution)/shard_map/all_to_all | solution.py:570
  135.8 10.0 %attend_frames.1 = (bf16[9,120,128]{2,1,0:T(8,128)(2,1)}, bf16[9,120,128]{2,1,0:T(8,128)(2,1)}, bf16[9,120,128]{2,1,0:T(8,128)(2,1)}, bf16[9,120,128]{2,1,0:T(8,...) custom-call(s32[2,24]{1,0:T(2,128)} %hc.13, ...), custom_call_target="tpu_custom_call" | custom-call | flops 2000000000 | bytes 6000000 | tf_op jit(solution)/shard_map/attend_frames/pallas_call | solution.py:454
  146.6 1.8 collective-permute-start.13
  150.5 17.1 %collective-permute-done.12.refs_1_ = bf16[9,120,128]{2,1,0:T(8,128)(2,1)S(1)} collective-permute-done((bf16[9,120,128]{2,1,0:T(8,128)(2,1)}, bf16[9,120,128]{2,1,0:T(8,128)(2,1)S(1)}, u32[]{:S(2)}, u32[]{:S(2)}) %collective-permute-start.12) | collective-permute-done | bytes 276512 | tf_op jit(solution)/shard_map/ppermute | solution.py:589
  167.6 1.9 collective-permute-start.16
  173.7 6.3 %unpack_spatial.1 = (bf16[2,1,120,3072]{3,2,1,0:T(8,128)(2,1)}, bf16[2,1,120,3072]{3,2,1,0:T(8,128)(2,1)}, bf16[2,1,120,3072]{3,2,1,0:T(8,128)(2,1)}) custom-call(s32[2,24]{1,0:T(2,128)} %hc.13, s32[2]{0:T(128)} %pad_add_fusion.place, bf16[16,544,128]{2,1,0:T(8,128)(2,1)} %copy-done.1), custom_call_target="tpu_custom_call" | custom-call | flops 5000000 | bytes 7000000 | tf_op jit(solution)/shard_map/unpack_spatial/pallas_call | solution.py:508
  180.0 3.8 %collective-permute-done.19.refs_6_ = bf16[9,120,128]{2,1,0:T(8,128)(2,1)S(1)} collective-permute-done((bf16[9,120,128]{2,1,0:T(8,128)(2,1)}, bf16[9,120,128]{2,1,0:T(8,128)(2,1)S(1)}, u32[]{:S(2)}, u32[]{:S(2)}) %collective-permute-start.19) | collective-permute-done | bytes 276512 | tf_op jit(solution)/shard_map/ppermute | solution.py:582
  183.8 5.5 %collective-permute-done.21.refs_7_ = bf16[9,120,128]{2,1,0:T(8,128)(2,1)} collective-permute-done((bf16[9,120,128]{2,1,0:T(8,128)(2,1)}, bf16[9,120,128]{2,1,0:T(8,128)(2,1)}, u32[]{:S(2)}, u32[]{:S(2)}) %collective-permute-start.21) | collective-permute-done | bytes 276512 | tf_op jit(solution)/shard_map/ppermute | solution.py:589
  189.3 4.2 %unpack_temporal.1 = (bf16[2,1,120,3072]{3,2,1,0:T(8,128)(2,1)}, bf16[2,1,120,3072]{3,2,1,0:T(8,128)(2,1)}, bf16[2,1,120,3072]{3,2,1,0:T(8,128)(2,1)}) custom-call(s32[2,24]{1,0:T(2,128)} %hc.13, s32[2]{0:T(128)} %pad_add_fusion.place, bf16[9,120,128]{2,1,0:T(8,128)(2,1)} %get-tuple-element.69.refs_0_, ...), custom_call_target="tpu_custom_call", output_to_operand_aliasing={{0}: (10, {}), {1}: (11, {}), {2}: (12, {})} | custom-call | bytes 5000000 | tf_op jit(solution)/shard_map/unpack_temporal/pallas_call | solution.py:549
  (67 shorter events, 19.4 us)
Async XLA Ops:
  7.6 53.7 %all-to-all-start = ((bf16[16,6,120,128]{3,2,1,0:T(8,128)(2,1)}), bf16[16,6,120,128]{3,2,1,0:T(8,128)(2,1)S(1)}, u32[]{:S(2)}, u32[]{:S(2)}) async-start(bf16[16,6,120,128]{3,2,1,0:T(8,128)(2,1)} %pack_spatial.1), calls=%async_computation | async-start | bytes 5898240 | tf_op jit(solution)/shard_map/all_to_all | solution.py:570
  23.6 11.6 %collective-permute-start = (bf16[12,120,128]{2,1,0:T(8,128)(2,1)}, bf16[12,120,128]{2,1,0:T(8,128)(2,1)S(1)}, u32[]{:S(2)}, u32[]{:S(2)}) collective-permute-start(bf16[12,120,128]{2,1,0:T(8,128)(2,1)} %get-tuple-element.44), channel_id=1, source_target_pairs={{0,16},{16,32},{32,48},{48,0},{64,80},{80,96},{96,112},{112,64},{1... | collective-permute-start | bytes 1105928 | tf_op jit(solution)/shard_map/ppermute | solution.py:582
  24.8 18.2 %collective-permute-start.1 = (bf16[12,120,128]{2,1,0:T(8,128)(2,1)}, bf16[12,120,128]{2,1,0:T(8,128)(2,1)S(1)}, u32[]{:S(2)}, u32[]{:S(2)}) collective-permute-start(bf16[12,120,128]{2,1,0:T(8,128)(2,1)} %get-tuple-element.45), channel_id=1, source_target_pairs={{0,16},{16,32},{32,48},{48,0},{64,80},{80,96},{96,112},{112,64},{1... | collective-permute-start | bytes 1105928 | tf_op jit(solution)/shard_map/ppermute | solution.py:582
  26.0 25.9 %collective-permute-start.2 = (bf16[12,120,128]{2,1,0:T(8,128)(2,1)}, bf16[12,120,128]{2,1,0:T(8,128)(2,1)S(1)}, u32[]{:S(2)}, u32[]{:S(2)}) collective-permute-start(bf16[12,120,128]{2,1,0:T(8,128)(2,1)} %get-tuple-element.46), channel_id=1, source_target_pairs={{0,32},{16,48},{32,0},{48,16},{64,96},{80,112},{96,64},{112,80},{1... | collective-permute-start | bytes 1105928 | tf_op jit(solution)/shard_map/ppermute | solution.py:582
  27.4 32.4 %collective-permute-start.3 = (bf16[12,120,128]{2,1,0:T(8,128)(2,1)}, bf16[12,120,128]{2,1,0:T(8,128)(2,1)S(1)}, u32[]{:S(2)}, u32[]{:S(2)}) collective-permute-start(bf16[12,120,128]{2,1,0:T(8,128)(2,1)} %get-tuple-element.47), channel_id=1, source_target_pairs={{0,32},{16,48},{32,0},{48,16},{64,96},{80,112},{96,64},{112,80},{1... | collective-permute-start | bytes 1105928 | tf_op jit(solution)/shard_map/ppermute | solution.py:582
  29.0 30.9 %collective-permute-start.4 = (bf16[12,120,128]{2,1,0:T(8,128)(2,1)}, bf16[12,120,128]{2,1,0:T(8,128)(2,1)S(1)}, u32[]{:S(2)}, u32[]{:S(2)}) collective-permute-start(bf16[12,120,128]{2,1,0:T(8,128)(2,1)} %get-tuple-element.48), channel_id=1, source_target_pairs={{0,48},{16,0},{32,16},{48,32},{64,112},{80,64},{96,80},{112,96},{1... | collective-permute-start | bytes 1105928 | tf_op jit(solution)/shard_map/ppermute | solution.py:582
  35.1 26.2 %collective-permute-start.5 = (bf16[12,120,128]{2,1,0:T(8,128)(2,1)}, bf16[12,120,128]{2,1,0:T(8,128)(2,1)}, u32[]{:S(2)}, u32[]{:S(2)}) collective-permute-start(bf16[12,120,128]{2,1,0:T(8,128)(2,1)} %get-tuple-element.49), channel_id=1, source_target_pairs={{0,48},{16,0},{32,16},{48,32},{64,112},{80,64},{96,80},{112,96},{1... | collective-permute-start | bytes 1105928 | tf_op jit(solution)/shard_map/ppermute | solution.py:582
  62.5 3.2 %collective-permute-start.6 = (bf16[16,2,120,128]{3,2,1,0:T(8,128)(2,1)S(1)}, bf16[16,2,120,128]{3,2,1,0:T(8,128)(2,1)}, u32[]{:S(2)}, u32[]{:S(2)}) collective-permute-start(bf16[16,2,120,128]{3,2,1,0:T(8,128)(2,1)S(1)} %slice.3.mine), channel_id=1, source_target_pairs={{0,1},{1,0},{2,3},{3,2},{4,5},{5,4},{6,7},{7,6},{8,9},{9,8},{10,11... | collective-permute-start | bytes 2949128 | tf_op jit(solution)/shard_map/ppermute | solution.py:602
  69.6 26.7 %collective-permute-start.7 = (bf16[16,184,128]{2,1,0:T(8,128)(2,1)}, bf16[16,184,128]{2,1,0:T(8,128)(2,1)S(1)}, u32[]{:S(2)}, u32[]{:S(2)}) collective-permute-start(bf16[16,184,128]{2,1,0:T(8,128)(2,1)} %get-tuple-element.52), channel_id=1, source_target_pairs={{0,1},{1,0},{2,3},{3,2},{4,5},{5,4},{6,7},{7,6},{8,9},{9,8},{10,11... | collective-permute-start | bytes 2261000 | tf_op jit(solution)/shard_map/ppermute | solution.py:604
  93.3 31.8 %collective-permute-start.8 = (bf16[12,120,128]{2,1,0:T(8,128)(2,1)}, bf16[12,120,128]{2,1,0:T(8,128)(2,1)S(1)}, u32[]{:S(2)}, u32[]{:S(2)}) collective-permute-start(bf16[12,120,128]{2,1,0:T(8,128)(2,1)} %get-tuple-element.54), channel_id=1, source_target_pairs={{0,64},{16,80},{32,96},{48,112},{64,0},{80,16},{96,32},{112,48},{1... | collective-permute-start | bytes 1105928 | tf_op jit(solution)/shard_map/ppermute | solution.py:589
  94.1 31.1 %collective-permute-start.9 = (bf16[12,120,128]{2,1,0:T(8,128)(2,1)}, bf16[12,120,128]{2,1,0:T(8,128)(2,1)S(1)}, u32[]{:S(2)}, u32[]{:S(2)}) collective-permute-start(bf16[12,120,128]{2,1,0:T(8,128)(2,1)} %copy-done.11), channel_id=1, source_target_pairs={{0,64},{16,80},{32,96},{48,112},{64,0},{80,16},{96,32},{112,48},{1... | collective-permute-start | bytes 1105928 | tf_op jit(solution)/shard_map/ppermute | solution.py:589
  94.8 30.4 %collective-permute-start.10 = (bf16[12,120,128]{2,1,0:T(8,128)(2,1)}, bf16[12,120,128]{2,1,0:T(8,128)(2,1)S(1)}, u32[]{:S(2)}, u32[]{:S(2)}) collective-permute-start(bf16[12,120,128]{2,1,0:T(8,128)(2,1)} %copy-done.12), channel_id=1, source_target_pairs={{0,64},{16,80},{32,96},{48,112},{64,0},{80,16},{96,32},{112,48},{1... | collective-permute-start | bytes 1105928 | tf_op jit(solution)/shard_map/ppermute | solution.py:589
  95.5 31.8 %collective-permute-start.11 = (bf16[12,120,128]{2,1,0:T(8,128)(2,1)}, bf16[12,120,128]{2,1,0:T(8,128)(2,1)S(1)}, u32[]{:S(2)}, u32[]{:S(2)}) collective-permute-start(bf16[12,120,128]{2,1,0:T(8,128)(2,1)} %collective-permute-done.5), channel_id=1, source_target_pairs={{0,64},{16,80},{32,96},{48,112},{64,0},{80,16},{96,32},{112,48},{1... | collective-permute-start | bytes 1105928 | tf_op jit(solution)/shard_map/ppermute | solution.py:589
  128.1 44.2 %all-to-all-start.1 = ((bf16[16,544,128]{2,1,0:T(8,128)(2,1)}), bf16[16,544,128]{2,1,0:T(8,128)(2,1)S(1)}, u32[]{:S(2)}, u32[]{:S(2)}) async-start(bf16[16,544,128]{2,1,0:T(8,128)(2,1)} %attend_own.1), calls=%async_computation.1 | async-start | bytes 4456448 | tf_op jit(solution)/shard_map/all_to_all | solution.py:570
  145.9 21.7 %collective-permute-start.12 = (bf16[9,120,128]{2,1,0:T(8,128)(2,1)}, bf16[9,120,128]{2,1,0:T(8,128)(2,1)S(1)}, u32[]{:S(2)}, u32[]{:S(2)}) collective-permute-start(bf16[9,120,128]{2,1,0:T(8,128)(2,1)} %get-tuple-element.70), channel_id=1, source_target_pairs={{0,64},{16,80},{32,96},{48,112},{64,0},{80,16},{96,32},{112,48},{1... | collective-permute-start | bytes 829448 | tf_op jit(solution)/shard_map/ppermute | solution.py:589
  146.6 22.9 %collective-permute-start.13 = (bf16[9,120,128]{2,1,0:T(8,128)(2,1)}, bf16[9,120,128]{2,1,0:T(8,128)(2,1)S(1)}, u32[]{:S(2)}, u32[]{:S(2)}) collective-permute-start(bf16[9,120,128]{2,1,0:T(8,128)(2,1)} %get-tuple-element.71), channel_id=1, source_target_pairs={{0,48},{16,0},{32,16},{48,32},{64,112},{80,64},{96,80},{112,96},{1... | collective-permute-start | bytes 829448 | tf_op jit(solution)/shard_map/ppermute | solution.py:582
  148.4 21.7 %collective-permute-start.14 = (bf16[9,120,128]{2,1,0:T(8,128)(2,1)}, bf16[9,120,128]{2,1,0:T(8,128)(2,1)}, u32[]{:S(2)}, u32[]{:S(2)}) collective-permute-start(bf16[9,120,128]{2,1,0:T(8,128)(2,1)} %get-tuple-element.72), channel_id=1, source_target_pairs={{0,48},{16,0},{32,16},{48,32},{64,112},{80,64},{96,80},{112,96},{1... | collective-permute-start | bytes 829448 | tf_op jit(solution)/shard_map/ppermute | solution.py:582
  148.8 22.1 %collective-permute-start.17 = (bf16[9,120,128]{2,1,0:T(8,128)(2,1)}, bf16[9,120,128]{2,1,0:T(8,128)(2,1)}, u32[]{:S(2)}, u32[]{:S(2)}) collective-permute-start(bf16[9,120,128]{2,1,0:T(8,128)(2,1)} %get-tuple-element.74), channel_id=1, source_target_pairs={{0,32},{16,48},{32,0},{48,16},{64,96},{80,112},{96,64},{112,80},{1... | collective-permute-start | bytes 829448 | tf_op jit(solution)/shard_map/ppermute | solution.py:582
  149.9 21.7 %collective-permute-start.20 = (bf16[9,120,128]{2,1,0:T(8,128)(2,1)}, bf16[9,120,128]{2,1,0:T(8,128)(2,1)}, u32[]{:S(2)}, u32[]{:S(2)}) collective-permute-start(bf16[9,120,128]{2,1,0:T(8,128)(2,1)} %get-tuple-element.76), channel_id=1, source_target_pairs={{0,16},{16,32},{32,48},{48,0},{64,80},{80,96},{96,112},{112,64},{1... | collective-permute-start | bytes 829448 | tf_op jit(solution)/shard_map/ppermute | solution.py:582
  167.6 12.3 %collective-permute-start.16 = (bf16[9,120,128]{2,1,0:T(8,128)(2,1)}, bf16[9,120,128]{2,1,0:T(8,128)(2,1)S(1)}, u32[]{:S(2)}, u32[]{:S(2)}) collective-permute-start(bf16[9,120,128]{2,1,0:T(8,128)(2,1)} %get-tuple-element.73), channel_id=1, source_target_pairs={{0,32},{16,48},{32,0},{48,16},{64,96},{80,112},{96,64},{112,80},{1... | collective-permute-start | bytes 829448 | tf_op jit(solution)/shard_map/ppermute | solution.py:582
  169.5 14.3 %collective-permute-start.19 = (bf16[9,120,128]{2,1,0:T(8,128)(2,1)}, bf16[9,120,128]{2,1,0:T(8,128)(2,1)S(1)}, u32[]{:S(2)}, u32[]{:S(2)}) collective-permute-start(bf16[9,120,128]{2,1,0:T(8,128)(2,1)} %get-tuple-element.75), channel_id=1, source_target_pairs={{0,16},{16,32},{32,48},{48,0},{64,80},{80,96},{96,112},{112,64},{1... | collective-permute-start | bytes 829448 | tf_op jit(solution)/shard_map/ppermute | solution.py:582
  170.1 13.7 %collective-permute-start.15 = (bf16[9,120,128]{2,1,0:T(8,128)(2,1)}, bf16[9,120,128]{2,1,0:T(8,128)(2,1)}, u32[]{:S(2)}, u32[]{:S(2)}) collective-permute-start(bf16[9,120,128]{2,1,0:T(8,128)(2,1)} %collective-permute-done.14), channel_id=1, source_target_pairs={{0,64},{16,80},{32,96},{48,112},{64,0},{80,16},{96,32},{112,48},{1... | collective-permute-start | bytes 829448 | tf_op jit(solution)/shard_map/ppermute | solution.py:589
  170.8 13.0 %collective-permute-start.18 = (bf16[9,120,128]{2,1,0:T(8,128)(2,1)}, bf16[9,120,128]{2,1,0:T(8,128)(2,1)}, u32[]{:S(2)}, u32[]{:S(2)}) collective-permute-start(bf16[9,120,128]{2,1,0:T(8,128)(2,1)} %collective-permute-done.17), channel_id=1, source_target_pairs={{0,64},{16,80},{32,96},{48,112},{64,0},{80,16},{96,32},{112,48},{1... | collective-permute-start | bytes 829448 | tf_op jit(solution)/shard_map/ppermute | solution.py:589
  171.6 17.8 %collective-permute-start.21 = (bf16[9,120,128]{2,1,0:T(8,128)(2,1)}, bf16[9,120,128]{2,1,0:T(8,128)(2,1)}, u32[]{:S(2)}, u32[]{:S(2)}) collective-permute-start(bf16[9,120,128]{2,1,0:T(8,128)(2,1)} %collective-permute-done.20), channel_id=1, source_target_pairs={{0,64},{16,80},{32,96},{48,112},{64,0},{80,16},{96,32},{112,48},{1... | collective-permute-start | bytes 829448 | tf_op jit(solution)/shard_map/ppermute | solution.py:589
  (17 other events, 138.3 us)

commit v2 on v1

--- a/solution.py
+++ b/solution.py
@@ -24,6 +24,7 @@
 QB = 512
 PADDED = 2048
 KB = 480
+STRIP = 16
 TP = 24
 GROUP = 4
 VMEM = 60 * 1024 * 1024
@@ -66,9 +67,10 @@
 
 
 def swapped(x):
-    up = pltpu.roll(x, W - 1, 1)
-    low = pltpu.roll(x, 1, 1)
-    return jnp.where(lane_ids(x.shape) % 2 == 0, up, low)
+    row = lax.broadcasted_iota(jnp.int32, (W, W), 0)
+    column = lax.broadcasted_iota(jnp.int32, (W, W), 1)
+    pairs = jnp.where((row ^ 1) == column, 1.0, 0.0).astype(BF16)
+    return jnp.dot(x.astype(BF16), pairs, preferred_element_type=F32)
 
 
 def merged(time_row, place_rows):
@@ -230,7 +232,7 @@
 
 
 def attend_body(q, k, v, g, ct, st, cp, sp, store, scratch):
-    qs, ks, vs, gs, kt, qt, gt, s_a, s_b, d_a, d_b, dk, dv, dq = scratch
+    qs, ks, vs, gs, kt, qt, gt, s_a, s_b, d_a, d_b, dk, dv, dq, dqt, p_ref, ds_ref = scratch
 
     def rows(j):
         return pl.ds(pl.multiple_of(j * KB, KB), KB)
@@ -262,60 +264,84 @@
 
     lax.fori_loop(0, PADDED // QB, turn, 0)
 
-    def products(i, j, top, refs):
+    def products(i, j, refs):
         s_ref, d_ref = refs
-        s = jnp.dot(ks[rows(j), :], qt[i], preferred_element_type=F32)
-        s_ref[rows(j), :] = s
+        s_ref[rows(j), :] = jnp.dot(ks[rows(j), :], qt[i], preferred_element_type=F32)
         d_ref[rows(j), :] = jnp.dot(vs[rows(j), :], gt[i], preferred_element_type=F32)
-        return jnp.maximum(top, jnp.max(s, 0, keepdims=True))
-
-    low = jnp.full((1, QB), -jnp.inf, F32)
-    zero = jnp.zeros((1, QB), F32)
+
+    def strips(j):
+        return [pl.ds(pl.multiple_of(j * KB + r, STRIP), STRIP) for r in range(0, KB, STRIP)]
+
+    def fold(op, total, strip):
+        for r in range(0, STRIP, 8):
+            total = op(total, strip[r : r + 8])
+        return total
+
+    def highest(j, top, refs):
+        for at in strips(j):
+            top = fold(jnp.maximum, top, refs[0][at, :])
+        return top
+
+    low = jnp.full((8, QB), -jnp.inf, F32)
+    zero = jnp.zeros((8, QB), F32)
 
     def block(i, after_i, top, refs, after_refs):
         s_ref, d_ref = refs
+        top = jnp.max(top, 0, keepdims=True) * SCALE2
 
         def sums(j, carry):
-            total, delta, after = carry
-            p = jnp.exp2((s_ref[rows(j), :] - top) * SCALE2)
-            total = total + jnp.sum(p, 0, keepdims=True)
-            delta = delta + jnp.sum(p * d_ref[rows(j), :], 0, keepdims=True)
-            return total, delta, products(after_i, j, after, after_refs)
-
-        total, delta, after = lax.fori_loop(0, CHUNKS, sums, (zero, zero, low))
-        delta = delta / total
-        shift = jnp.log2(total)
-
-        def grads(j, dqt):
-            p = jnp.exp2((s_ref[rows(j), :] - top) * SCALE2 - shift)
-            ds = (p * ((d_ref[rows(j), :] - delta) * SCALE)).astype(BF16)
-            dv[rows(j), :] += jnp.dot(
-                p.astype(BF16), gs[queries(i), :], preferred_element_type=F32
-            )
-            dk[rows(j), :] += jnp.dot(ds, qs[queries(i), :], preferred_element_type=F32)
-            return dqt + jnp.dot(kt[j], ds, preferred_element_type=F32)
-
-        dqt = lax.fori_loop(0, CHUNKS, grads, jnp.zeros((W, QB), F32))
-        dq[queries(i), :] = dqt.T
+            total, delta = carry
+            products(after_i, j, after_refs)
+            for at in strips(j):
+                p = jnp.exp2(s_ref[at, :] * SCALE2 - top)
+                total = fold(jnp.add, total, p)
+                delta = fold(jnp.add, delta, p * d_ref[at, :])
+            return total, delta
+
+        total, delta = lax.fori_loop(0, CHUNKS, sums, (zero, zero))
+        total = jnp.sum(total, 0, keepdims=True)
+        delta = jnp.sum(delta, 0, keepdims=True) / total * SCALE
+        shift = top + jnp.log2(total)
+        dqt[...] = jnp.zeros_like(dqt)
+
+        def grads(j, after):
+            for r, at in enumerate(strips(j)):
+                p = jnp.exp2(s_ref[at, :] * SCALE2 - shift)
+                ds = p * (d_ref[at, :] * SCALE - delta)
+                to = slice(r * STRIP, (r + 1) * STRIP)
+                p_ref[to, :] = p.astype(BF16)
+                ds_ref[to, :] = ds.astype(BF16)
+            dv[rows(j), :] += jnp.dot(p_ref[...], gs[queries(i), :], preferred_element_type=F32)
+            dk[rows(j), :] += jnp.dot(ds_ref[...], qs[queries(i), :], preferred_element_type=F32)
+            dqt[...] += jnp.dot(kt[j], ds_ref[...], preferred_element_type=F32)
+            return highest(j, after, after_refs)
+
+        after = lax.fori_loop(0, CHUNKS, grads, low)
+        dq[queries(i), :] = dqt[...].T
         return after
 
     one, two = (s_a, d_a), (s_b, d_b)
-    top = lax.fori_loop(0, CHUNKS, lambda j, t: products(0, j, t, one), low)
+
+    def start(j, top):
+        products(0, j, one)
+        return highest(j, top, one)
 
     def blocks(n, top):
         top = block(2 * n, 2 * n + 1, top, one, two)
         return block(2 * n + 1, jnp.minimum(2 * n + 2, PADDED // QB - 1), top, two, one)
 
-    lax.fori_loop(0, PADDED // QB // 2, blocks, top)
-
-    def finish(b, carry):
-        at = pl.ds(pl.multiple_of(b * ROWS, ROWS), ROWS)
-        cosine = merged(ct, cp[at, :])
-        sine = merged(st, sp[at, :])
-        store(b, unrotate(dq[at, :], cosine, sine), unrotate(dk[at, :], cosine, sine), dv[at, :])
+    lax.fori_loop(0, PADDED // QB // 2, blocks, lax.fori_loop(0, CHUNKS, start, low))
+
+    def finish(n, carry):
+        for b in [n * 4 + u for u in range(4)]:
+            at = pl.ds(pl.multiple_of(b * ROWS, ROWS), ROWS)
+            cosine = merged(ct, cp[at, :])
+            sine = merged(st, sp[at, :])
+            gq = unrotate(dq[at, :], cosine, sine)
+            store(b, gq, unrotate(dk[at, :], cosine, sine), dv[at, :])
         return carry
 
-    lax.fori_loop(0, SPACES, finish, 0)
+    lax.fori_loop(0, SPACES // 4, finish, 0)
 
 
 def attend_scratch():
@@ -326,7 +352,8 @@
         + [pltpu.VMEM((PADDED // QB, W, QB), BF16)] * 2
         + [pltpu.VMEM((POSITIONS, QB), F32)] * 4
         + [pltpu.VMEM((POSITIONS, W), F32)] * 2
-        + [pltpu.VMEM((PADDED, W), F32)]
+        + [pltpu.VMEM((PADDED, W), F32), pltpu.VMEM((W, QB), F32)]
+        + [pltpu.VMEM((KB, QB), BF16)] * 2
     )
 
 
@@ -601,11 +628,12 @@
     mine = got_s[:, 4:6]
     other = lax.ppermute(mine, "space", SWAP)
     kept, give = attend_shared(meta, mine, other, tabs)
+    kept, give, got_t[1], got_t[3] = lax.optimization_barrier((kept, give, got_t[1], got_t[3]))
     given = lax.ppermute(give, "space", SWAP)
     back_s = attend_own(meta, got_s, kept, given, tabs)
     back_s, *got_t = lax.optimization_barrier((back_s, *got_t))
     home_s = exchange(back_s)
-    home_t = along_z(along_x(attend_frames(meta, got_t, tabs), -1))
+    home_t = along_x(along_z(attend_frames(meta, got_t, tabs)), -1)
     partial = unpack_spatial(meta, home_s)
     return tuple(unpack_temporal(meta, home_t, partial))
 

time: 195 us -> 193 us (0.990)
  starting transfers between devices: 62 us -> 50.3 us
  waiting for transfers between devices: 59.1 us -> 69.1 us
    ppermute x8, waiting for transfers between devices: 24.8 us -> 38.7 us  [along_z(): lax.ppermute(x, 'frame', pairs)]
    ppermute x1, starting transfers between devices: 23.7 us -> 10 us  [on_device(): given = lax.ppermute(give, 'space', SWAP)]
    ppermute x12, waiting for transfers between devices: 32 us -> 28.9 us  [move(): return lax.ppermute(part, 'frame', pairs)]
    ppermute x12, starting transfers between devices: 14.5 us -> 17 us  [move(): return lax.ppermute(part, 'frame', pairs)]
    pallas_call x1, Pallas kernels: 10 us -> 12.1 us  [attend_frames(): pl.pallas_call(frames_body, grid_spec=pltpu.PrefetchScalarGridSpec(num_sc...]
    pallas_call x1, Pallas kernels: 28 us -> 26 us  [attend_own(): pl.pallas_call(own_body, grid_spec=pltpu.PrefetchScalarGridSpec(num_scala...]
    unnamed x34 -> x30, local copies, waits for them, and re-layouts: 5.57 us -> 5.58 us
  transfers between devices with their start and end apart: 24 -> 24, of which waited for: 9 -> 13; matrix products, arithmetic and copies ran while one was open for 0% -> 0% of each run, Pallas kernels for 26% -> 29%
where the time goes in v2:
time: 193 us
  waiting for transfers between devices  69.1 us (36%)
  Pallas kernels  65.9 us (34%)
  starting transfers between devices  50.3 us (26%)
  local copies, waits for them, and re-layouts  5.65 us (3%)
    ppermute x8, waiting for transfers between devices, along_z(): lax.ppermute(x, 'frame', pairs)  38.7 us
    ppermute x12, waiting for transfers between devices, move(): return lax.ppermute(part, 'frame', pairs)  28.9 us
    pallas_call x1, Pallas kernels, attend_own(): pl.pallas_call(own_body, grid_spec=pltpu.PrefetchScalarGridSpec(num_scala...  26 us
    ppermute x12, starting transfers between devices, move(): return lax.ppermute(part, 'frame', pairs)  17 us
    all_to_all x2, starting transfers between devices, exchange(): return lax.all_to_all(x, 'space', split_axis=0, concat_axis=0, tiled=True)  16.5 us
    pallas_call x1, Pallas kernels, attend_frames(): pl.pallas_call(frames_body, grid_spec=pltpu.PrefetchScalarGridSpec(num_sc...  12.1 us
    ppermute x1, starting transfers between devices, on_device(): given = lax.ppermute(give, 'space', SWAP)  10 us
    pallas_call x1, Pallas kernels, pack_temporal(): pl.pallas_call(pack_temporal_body, grid_spec=pltpu.PrefetchScalarGridSpec...  6.91 us
  transfers between devices with their start and end apart: 24, of which 13 were waited for; matrix products, arithmetic and copies ran while one was open for 0% of the time, Pallas kernels for 29%

profile of v2, /device:TPU:1, one launch (start us, length us, event | category | flops | bytes accessed | tf_op | source)
XLA Modules:
  0.0 192.6 jit_solution(18232084210315412528)
XLA Ops:
  1.3 6.5 %pack_spatial.1 = bf16[16,6,120,128]{3,2,1,0:T(8,128)(2,1)} custom-call(s32[2,24]{1,0:T(2,128)} %hc.13, s32[2]{0:T(128)} %pad_add_fusion.place, bf16[2,1,120,3072]{3,2,1,0:T(8,128)(2,1)} %q.3, bf16[2,1,120,3072]{3,2,1,0:T(8,128)(2,1)} %k.3, bf16[2,1,120,3072]{3,2,1,0:T(8,128)(2,1)} %v.3, bf16[2,1,120,3072]{3,2,1,0:T(8,128)(2,1)} %g.3, ...), custom_call_target="tpu_custom_call" | custom-call | flops 20000000 | bytes 9000000 | tf_op jit(solution)/shard_map/pack_spatial/pallas_call | solution.py:159
  7.7 9.3 %all-to-all-start = ((bf16[16,6,120,128]{3,2,1,0:T(8,128)(2,1)}), bf16[16,6,120,128]{3,2,1,0:T(8,128)(2,1)S(1)}, u32[]{:S(2)}, u32[]{:S(2)}) async-start(bf16[16,6,120,128]{3,2,1,0:T(8,128)(2,1)} %pack_spatial.1), calls=%async_computation | async-start | bytes 5898240 | tf_op jit(solution)/shard_map/all_to_all | solution.py:597
  17.0 6.9 %pack_temporal.1 = (bf16[12,120,128]{2,1,0:T(8,128)(2,1)}, bf16[12,120,128]{2,1,0:T(8,128)(2,1)}, bf16[12,120,128]{2,1,0:T(8,128)(2,1)}, bf16[12,120,128]{2,1,0:...) custom-call(s32[2,24]{1,0:T(2,128)} %hc.13, ...), custom_call_target="tpu_custom_call" | custom-call | flops 20000000 | bytes 9000000 | tf_op jit(solution)/shard_map/pack_temporal/pallas_call | solution.py:210
  30.8 4.7 %collective-permute-done.refs_2_ = bf16[12,120,128]{2,1,0:T(8,128)(2,1)S(1)} collective-permute-done((bf16[12,120,128]{2,1,0:T(8,128)(2,1)}, bf16[12,120,128]{2,1,0:T(8,128)(2,1)S(1)}, u32[]{:S(2)}, u32[]{:S(2)}) %collective-permute-start) | collective-permute-done | bytes 368672 | tf_op jit(solution)/shard_map/ppermute | solution.py:609
  36.8 6.7 %collective-permute-done.1 = bf16[12,120,128]{2,1,0:T(8,128)(2,1)} collective-permute-done((bf16[12,120,128]{2,1,0:T(8,128)(2,1)}, bf16[12,120,128]{2,1,0:T(8,128)(2,1)}, u32[]{:S(2)}, u32[]{:S(2)}) %collective-permute-start.1) | collective-permute-done | bytes 368672 | tf_op jit(solution)/shard_map/ppermute | solution.py:609
  43.5 8.8 %collective-permute-done.2.refs_4_ = bf16[12,120,128]{2,1,0:T(8,128)(2,1)S(1)} collective-permute-done((bf16[12,120,128]{2,1,0:T(8,128)(2,1)}, bf16[12,120,128]{2,1,0:T(8,128)(2,1)S(1)}, u32[]{:S(2)}, u32[]{:S(2)}) %collective-permute-start.2) | collective-permute-done | bytes 368672 | tf_op jit(solution)/shard_map/ppermute | solution.py:609
  52.3 7.9 %collective-permute-done.3 = bf16[12,120,128]{2,1,0:T(8,128)(2,1)S(1)} collective-permute-done((bf16[12,120,128]{2,1,0:T(8,128)(2,1)}, bf16[12,120,128]{2,1,0:T(8,128)(2,1)S(1)}, u32[]{:S(2)}, u32[]{:S(2)}) %collective-permute-start.3) | collective-permute-done | bytes 368672 | tf_op jit(solution)/shard_map/ppermute | solution.py:609
  66.0 3.9 %attend_shared.1 = (bf16[16,184,128]{2,1,0:T(8,128)(2,1)}, bf16[16,184,128]{2,1,0:T(8,128)(2,1)}) custom-call(s32[2,24]{1,0:T(2,128)} %hc.13, s32[2]{0:T(128)} %pad_add_fusion.place, bf16[16,2,120,128]{3,2,1,0:T(8,128)(2,1)} %copy-done.2, bf16[16,2,120,128]{3,2,1,0:T(8,128)(2,1)} %collective-permute-done.6.other, f32[8,128]{1,0:T(8,128)} %constant.17.clone.ct.refs_8_, ...), custom_call_target="tpu_custom_call" | custom-call | flops 4718592000 | bytes 6000000 | tf_op jit(solution)/shard_map/attend_shared/pallas_call | solution.py:419
  69.9 3.9 %collective-permute-done.7.refs_1_ = bf16[12,120,128]{2,1,0:T(8,128)(2,1)} collective-permute-done((bf16[12,120,128]{2,1,0:T(8,128)(2,1)S(1)}, bf16[12,120,128]{2,1,0:T(8,128)(2,1)}, u32[]{:S(2)}, u32[]{:S(2)}) %collective-permute-start.7) | collective-permute-done | bytes 368672 | tf_op jit(solution)/shard_map/ppermute | solution.py:616
  73.8 7.9 %collective-permute-done.8.refs_3_ = bf16[12,120,128]{2,1,0:T(8,128)(2,1)} collective-permute-done((bf16[12,120,128]{2,1,0:T(8,128)(2,1)}, bf16[12,120,128]{2,1,0:T(8,128)(2,1)}, u32[]{:S(2)}, u32[]{:S(2)}) %collective-permute-start.8) | collective-permute-done | bytes 368672 | tf_op jit(solution)/shard_map/ppermute | solution.py:616
  81.7 10.0 %collective-permute-start.9 = (bf16[16,184,128]{2,1,0:T(8,128)(2,1)}, bf16[16,184,128]{2,1,0:T(8,128)(2,1)S(1)}, u32[]{:S(2)}, u32[]{:S(2)}) collective-permute-start(bf16[16,184,128]{2,1,0:T(8,128)(2,1)} %get-tuple-element.60), channel_id=1, source_target_pairs={{0,1},{1,0},{2,3},{3,2},{4,5},{5,4},{6,7},{7,6},{8,9},{9,8},{10,11... | collective-permute-start | bytes 2261000 | tf_op jit(solution)/shard_map/ppermute | solution.py:632
  94.7 26.0 %attend_own.1 = bf16[16,544,128]{2,1,0:T(8,128)(2,1)} custom-call(s32[2,24]{1,0:T(2,128)} %hc.13, s32[2]{0:T(128)} %pad_add_fusion.place, bf16[16,6,120,128]{3,2,1,0:T(8,128)(2,1)} %copy-done, bf16[16,184,128]{2,1,0:T(8,128)(2,1)} %get-tuple-element.59.kept, bf16[16,184,128]{2,1,0:T(8,128)(2,1)} %copy-done.3, f32[8,128]{1,0:T(8,128)} %constant.17.clone.ct.refs_8_, ...), custom_call_target="tpu_custom_call" | custom-call | bytes 6000000 | tf_op jit(solution)/shard_map/attend_own/pallas_call | solution.py:400
  121.6 7.2 %all-to-all-start.1 = ((bf16[16,544,128]{2,1,0:T(8,128)(2,1)}), bf16[16,544,128]{2,1,0:T(8,128)(2,1)S(1)}, u32[]{:S(2)}, u32[]{:S(2)}) async-start(bf16[16,544,128]{2,1,0:T(8,128)(2,1)} %attend_own.1), calls=%async_computation.1 | async-start | bytes 4456448 | tf_op jit(solution)/shard_map/all_to_all | solution.py:597
  128.8 12.1 %attend_frames.1 = (bf16[9,120,128]{2,1,0:T(8,128)(2,1)}, bf16[9,120,128]{2,1,0:T(8,128)(2,1)}, bf16[9,120,128]{2,1,0:T(8,128)(2,1)}, bf16[9,120,128]{2,1,0:T(8,...) custom-call(s32[2,24]{1,0:T(2,128)} %hc.13, ...), custom_call_target="tpu_custom_call" | custom-call | flops 2000000000 | bytes 6000000 | tf_op jit(solution)/shard_map/attend_frames/pallas_call | solution.py:481
  141.7 1.8 collective-permute-start.13
  145.6 15.0 %collective-permute-done.12.refs_1_ = bf16[9,120,128]{2,1,0:T(8,128)(2,1)S(1)} collective-permute-done((bf16[9,120,128]{2,1,0:T(8,128)(2,1)}, bf16[9,120,128]{2,1,0:T(8,128)(2,1)S(1)}, u32[]{:S(2)}, u32[]{:S(2)}) %collective-permute-start.12) | collective-permute-done | bytes 276512 | tf_op jit(solution)/shard_map/ppermute | solution.py:616
  160.6 1.8 collective-permute-start.16
  163.0 3.7 %collective-permute-done.14 = bf16[9,120,128]{2,1,0:T(8,128)(2,1)} collective-permute-done((bf16[9,120,128]{2,1,0:T(8,128)(2,1)}, bf16[9,120,128]{2,1,0:T(8,128)(2,1)}, u32[]{:S(2)}, u32[]{:S(2)}) %collective-permute-start.14) | collective-permute-done | bytes 276512 | tf_op jit(solution)/shard_map/ppermute | solution.py:616
  166.6 1.8 collective-permute-start.15
  168.4 4.2 %collective-permute-done.17 = bf16[9,120,128]{2,1,0:T(8,128)(2,1)} collective-permute-done((bf16[9,120,128]{2,1,0:T(8,128)(2,1)}, bf16[9,120,128]{2,1,0:T(8,128)(2,1)}, u32[]{:S(2)}, u32[]{:S(2)}) %collective-permute-start.17) | collective-permute-done | bytes 276512 | tf_op jit(solution)/shard_map/ppermute | solution.py:616
  172.6 1.8 collective-permute-start.18
  174.4 4.1 %collective-permute-done.20 = bf16[9,120,128]{2,1,0:T(8,128)(2,1)} collective-permute-done((bf16[9,120,128]{2,1,0:T(8,128)(2,1)}, bf16[9,120,128]{2,1,0:T(8,128)(2,1)}, u32[]{:S(2)}, u32[]{:S(2)}) %collective-permute-start.20) | collective-permute-done | bytes 276512 | tf_op jit(solution)/shard_map/ppermute | solution.py:616
  181.1 6.3 %unpack_spatial.1 = (bf16[2,1,120,3072]{3,2,1,0:T(8,128)(2,1)}, bf16[2,1,120,3072]{3,2,1,0:T(8,128)(2,1)}, bf16[2,1,120,3072]{3,2,1,0:T(8,128)(2,1)}) custom-call(s32[2,24]{1,0:T(2,128)} %hc.13, s32[2]{0:T(128)} %pad_add_fusion.place, bf16[16,544,128]{2,1,0:T(8,128)(2,1)} %copy-done.1), custom_call_target="tpu_custom_call" | custom-call | flops 5000000 | bytes 7000000 | tf_op jit(solution)/shard_map/unpack_spatial/pallas_call | solution.py:535
  188.2 4.2 %unpack_temporal.1 = (bf16[2,1,120,3072]{3,2,1,0:T(8,128)(2,1)}, bf16[2,1,120,3072]{3,2,1,0:T(8,128)(2,1)}, bf16[2,1,120,3072]{3,2,1,0:T(8,128)(2,1)}) custom-call(s32[2,24]{1,0:T(2,128)} %hc.13, s32[2]{0:T(128)} %pad_add_fusion.place, bf16[9,120,128]{2,1,0:T(8,128)(2,1)} %get-tuple-element.77.refs_0_, ...), custom_call_target="tpu_custom_call", output_to_operand_aliasing={{0}: (10, {}), {1}: (11, {}), {2}: (12, {})} | custom-call | bytes 5000000 | tf_op jit(solution)/shard_map/unpack_temporal/pallas_call | solution.py:576
  (63 shorter events, 25.1 us)
Async XLA Ops:
  7.7 54.0 %all-to-all-start = ((bf16[16,6,120,128]{3,2,1,0:T(8,128)(2,1)}), bf16[16,6,120,128]{3,2,1,0:T(8,128)(2,1)S(1)}, u32[]{:S(2)}, u32[]{:S(2)}) async-start(bf16[16,6,120,128]{3,2,1,0:T(8,128)(2,1)} %pack_spatial.1), calls=%async_computation | async-start | bytes 5898240 | tf_op jit(solution)/shard_map/all_to_all | solution.py:597
  23.9 11.6 %collective-permute-start = (bf16[12,120,128]{2,1,0:T(8,128)(2,1)}, bf16[12,120,128]{2,1,0:T(8,128)(2,1)S(1)}, u32[]{:S(2)}, u32[]{:S(2)}) collective-permute-start(bf16[12,120,128]{2,1,0:T(8,128)(2,1)} %get-tuple-element.48), channel_id=1, source_target_pairs={{0,16},{16,32},{32,48},{48,0},{64,80},{80,96},{96,112},{112,64},{1... | collective-permute-start | bytes 1105928 | tf_op jit(solution)/shard_map/ppermute | solution.py:609
  25.1 18.4 %collective-permute-start.1 = (bf16[12,120,128]{2,1,0:T(8,128)(2,1)}, bf16[12,120,128]{2,1,0:T(8,128)(2,1)}, u32[]{:S(2)}, u32[]{:S(2)}) collective-permute-start(bf16[12,120,128]{2,1,0:T(8,128)(2,1)} %get-tuple-element.49), channel_id=1, source_target_pairs={{0,16},{16,32},{32,48},{48,0},{64,80},{80,96},{96,112},{112,64},{1... | collective-permute-start | bytes 1105928 | tf_op jit(solution)/shard_map/ppermute | solution.py:609
  26.4 25.9 %collective-permute-start.2 = (bf16[12,120,128]{2,1,0:T(8,128)(2,1)}, bf16[12,120,128]{2,1,0:T(8,128)(2,1)S(1)}, u32[]{:S(2)}, u32[]{:S(2)}) collective-permute-start(bf16[12,120,128]{2,1,0:T(8,128)(2,1)} %get-tuple-element.50), channel_id=1, source_target_pairs={{0,32},{16,48},{32,0},{48,16},{64,96},{80,112},{96,64},{112,80},{1... | collective-permute-start | bytes 1105928 | tf_op jit(solution)/shard_map/ppermute | solution.py:609
  27.8 32.4 %collective-permute-start.3 = (bf16[12,120,128]{2,1,0:T(8,128)(2,1)}, bf16[12,120,128]{2,1,0:T(8,128)(2,1)S(1)}, u32[]{:S(2)}, u32[]{:S(2)}) collective-permute-start(bf16[12,120,128]{2,1,0:T(8,128)(2,1)} %get-tuple-element.51), channel_id=1, source_target_pairs={{0,32},{16,48},{32,0},{48,16},{64,96},{80,112},{96,64},{112,80},{1... | collective-permute-start | bytes 1105928 | tf_op jit(solution)/shard_map/ppermute | solution.py:609
  29.3 30.9 %collective-permute-start.4 = (bf16[12,120,128]{2,1,0:T(8,128)(2,1)}, bf16[12,120,128]{2,1,0:T(8,128)(2,1)S(1)}, u32[]{:S(2)}, u32[]{:S(2)}) collective-permute-start(bf16[12,120,128]{2,1,0:T(8,128)(2,1)} %get-tuple-element.52), channel_id=1, source_target_pairs={{0,48},{16,0},{32,16},{48,32},{64,112},{80,64},{96,80},{112,96},{1... | collective-permute-start | bytes 1105928 | tf_op jit(solution)/shard_map/ppermute | solution.py:609
  35.5 26.2 %collective-permute-start.5 = (bf16[12,120,128]{2,1,0:T(8,128)(2,1)}, bf16[12,120,128]{2,1,0:T(8,128)(2,1)}, u32[]{:S(2)}, u32[]{:S(2)}) collective-permute-start(bf16[12,120,128]{2,1,0:T(8,128)(2,1)} %get-tuple-element.53), channel_id=1, source_target_pairs={{0,48},{16,0},{32,16},{48,32},{64,112},{80,64},{96,80},{112,96},{1... | collective-permute-start | bytes 1105928 | tf_op jit(solution)/shard_map/ppermute | solution.py:609
  62.8 3.2 %collective-permute-start.6 = (bf16[16,2,120,128]{3,2,1,0:T(8,128)(2,1)S(1)}, bf16[16,2,120,128]{3,2,1,0:T(8,128)(2,1)}, u32[]{:S(2)}, u32[]{:S(2)}) collective-permute-start(bf16[16,2,120,128]{3,2,1,0:T(8,128)(2,1)S(1)} %slice.3.mine), channel_id=1, source_target_pairs={{0,1},{1,0},{2,3},{3,2},{4,5},{5,4},{6,7},{7,6},{8,9},{9,8},{10,11... | collective-permute-start | bytes 2949128 | tf_op jit(solution)/shard_map/ppermute | solution.py:629
  63.7 10.1 %collective-permute-start.7 = (bf16[12,120,128]{2,1,0:T(8,128)(2,1)S(1)}, bf16[12,120,128]{2,1,0:T(8,128)(2,1)}, u32[]{:S(2)}, u32[]{:S(2)}) collective-permute-start(bf16[12,120,128]{2,1,0:T(8,128)(2,1)S(1)} %copy-done.12), channel_id=1, source_target_pairs={{0,64},{16,80},{32,96},{48,112},{64,0},{80,16},{96,32},{112,48},{1... | collective-permute-start | bytes 1105928 | tf_op jit(solution)/shard_map/ppermute | solution.py:616
  64.4 17.3 %collective-permute-start.8 = (bf16[12,120,128]{2,1,0:T(8,128)(2,1)}, bf16[12,120,128]{2,1,0:T(8,128)(2,1)}, u32[]{:S(2)}, u32[]{:S(2)}) collective-permute-start(bf16[12,120,128]{2,1,0:T(8,128)(2,1)} %collective-permute-done.1), channel_id=1, source_target_pairs={{0,64},{16,80},{32,96},{48,112},{64,0},{80,16},{96,32},{112,48},{1... | collective-permute-start | bytes 1105928 | tf_op jit(solution)/shard_map/ppermute | solution.py:616
  81.7 12.1 %collective-permute-start.9 = (bf16[16,184,128]{2,1,0:T(8,128)(2,1)}, bf16[16,184,128]{2,1,0:T(8,128)(2,1)S(1)}, u32[]{:S(2)}, u32[]{:S(2)}) collective-permute-start(bf16[16,184,128]{2,1,0:T(8,128)(2,1)} %get-tuple-element.60), channel_id=1, source_target_pairs={{0,1},{1,0},{2,3},{3,2},{4,5},{5,4},{6,7},{7,6},{8,9},{9,8},{10,11... | collective-permute-start | bytes 2261000 | tf_op jit(solution)/shard_map/ppermute | solution.py:632
  91.7 29.0 %collective-permute-start.10 = (bf16[12,120,128]{2,1,0:T(8,128)(2,1)}, bf16[12,120,128]{2,1,0:T(8,128)(2,1)S(1)}, u32[]{:S(2)}, u32[]{:S(2)}) collective-permute-start(bf16[12,120,128]{2,1,0:T(8,128)(2,1)} %copy-done.11), channel_id=1, source_target_pairs={{0,64},{16,80},{32,96},{48,112},{64,0},{80,16},{96,32},{112,48},{1... | collective-permute-start | bytes 1105928 | tf_op jit(solution)/shard_map/ppermute | solution.py:616
  92.5 28.2 %collective-permute-start.11 = (bf16[12,120,128]{2,1,0:T(8,128)(2,1)}, bf16[12,120,128]{2,1,0:T(8,128)(2,1)S(1)}, u32[]{:S(2)}, u32[]{:S(2)}) collective-permute-start(bf16[12,120,128]{2,1,0:T(8,128)(2,1)} %collective-permute-done.5), channel_id=1, source_target_pairs={{0,64},{16,80},{32,96},{48,112},{64,0},{80,16},{96,32},{112,48},{1... | collective-permute-start | bytes 1105928 | tf_op jit(solution)/shard_map/ppermute | solution.py:616
  121.6 58.1 %all-to-all-start.1 = ((bf16[16,544,128]{2,1,0:T(8,128)(2,1)}), bf16[16,544,128]{2,1,0:T(8,128)(2,1)S(1)}, u32[]{:S(2)}, u32[]{:S(2)}) async-start(bf16[16,544,128]{2,1,0:T(8,128)(2,1)} %attend_own.1), calls=%async_computation.1 | async-start | bytes 4456448 | tf_op jit(solution)/shard_map/all_to_all | solution.py:597
  141.0 19.6 %collective-permute-start.12 = (bf16[9,120,128]{2,1,0:T(8,128)(2,1)}, bf16[9,120,128]{2,1,0:T(8,128)(2,1)S(1)}, u32[]{:S(2)}, u32[]{:S(2)}) collective-permute-start(bf16[9,120,128]{2,1,0:T(8,128)(2,1)} %get-tuple-element.78), channel_id=1, source_target_pairs={{0,64},{16,80},{32,96},{48,112},{64,0},{80,16},{96,32},{112,48},{1... | collective-permute-start | bytes 829448 | tf_op jit(solution)/shard_map/ppermute | solution.py:616
  141.7 20.7 %collective-permute-start.13 = (bf16[9,120,128]{2,1,0:T(8,128)(2,1)}, bf16[9,120,128]{2,1,0:T(8,128)(2,1)S(1)}, u32[]{:S(2)}, u32[]{:S(2)}) collective-permute-start(bf16[9,120,128]{2,1,0:T(8,128)(2,1)} %get-tuple-element.79), channel_id=1, source_target_pairs={{0,48},{16,0},{32,16},{48,32},{64,112},{80,64},{96,80},{112,96},{1... | collective-permute-start | bytes 829448 | tf_op jit(solution)/shard_map/ppermute | solution.py:609
  143.5 23.2 %collective-permute-start.14 = (bf16[9,120,128]{2,1,0:T(8,128)(2,1)}, bf16[9,120,128]{2,1,0:T(8,128)(2,1)}, u32[]{:S(2)}, u32[]{:S(2)}) collective-permute-start(bf16[9,120,128]{2,1,0:T(8,128)(2,1)} %get-tuple-element.80), channel_id=1, source_target_pairs={{0,64},{16,80},{32,96},{48,112},{64,0},{80,16},{96,32},{112,48},{1... | collective-permute-start | bytes 829448 | tf_op jit(solution)/shard_map/ppermute | solution.py:616
  144.2 28.4 %collective-permute-start.17 = (bf16[9,120,128]{2,1,0:T(8,128)(2,1)}, bf16[9,120,128]{2,1,0:T(8,128)(2,1)}, u32[]{:S(2)}, u32[]{:S(2)}) collective-permute-start(bf16[9,120,128]{2,1,0:T(8,128)(2,1)} %get-tuple-element.82), channel_id=1, source_target_pairs={{0,64},{16,80},{32,96},{48,112},{64,0},{80,16},{96,32},{112,48},{1... | collective-permute-start | bytes 829448 | tf_op jit(solution)/shard_map/ppermute | solution.py:616
  144.9 33.5 %collective-permute-start.20 = (bf16[9,120,128]{2,1,0:T(8,128)(2,1)}, bf16[9,120,128]{2,1,0:T(8,128)(2,1)}, u32[]{:S(2)}, u32[]{:S(2)}) collective-permute-start(bf16[9,120,128]{2,1,0:T(8,128)(2,1)} %get-tuple-element.84), channel_id=1, source_target_pairs={{0,64},{16,80},{32,96},{48,112},{64,0},{80,16},{96,32},{112,48},{1... | collective-permute-start | bytes 829448 | tf_op jit(solution)/shard_map/ppermute | solution.py:616
  160.6 26.7 %collective-permute-start.16 = (bf16[9,120,128]{2,1,0:T(8,128)(2,1)}, bf16[9,120,128]{2,1,0:T(8,128)(2,1)S(1)}, u32[]{:S(2)}, u32[]{:S(2)}) collective-permute-start(bf16[9,120,128]{2,1,0:T(8,128)(2,1)} %get-tuple-element.81), channel_id=1, source_target_pairs={{0,32},{16,48},{32,0},{48,16},{64,96},{80,112},{96,64},{112,80},{1... | collective-permute-start | bytes 829448 | tf_op jit(solution)/shard_map/ppermute | solution.py:609
  162.4 24.9 %collective-permute-start.19 = (bf16[9,120,128]{2,1,0:T(8,128)(2,1)}, bf16[9,120,128]{2,1,0:T(8,128)(2,1)S(1)}, u32[]{:S(2)}, u32[]{:S(2)}) collective-permute-start(bf16[9,120,128]{2,1,0:T(8,128)(2,1)} %get-tuple-element.83), channel_id=1, source_target_pairs={{0,16},{16,32},{32,48},{48,0},{64,80},{80,96},{96,112},{112,64},{1... | collective-permute-start | bytes 829448 | tf_op jit(solution)/shard_map/ppermute | solution.py:609
  166.6 20.7 %collective-permute-start.15 = (bf16[9,120,128]{2,1,0:T(8,128)(2,1)}, bf16[9,120,128]{2,1,0:T(8,128)(2,1)}, u32[]{:S(2)}, u32[]{:S(2)}) collective-permute-start(bf16[9,120,128]{2,1,0:T(8,128)(2,1)} %collective-permute-done.14), channel_id=1, source_target_pairs={{0,48},{16,0},{32,16},{48,32},{64,112},{80,64},{96,80},{112,96},{1... | collective-permute-start | bytes 829448 | tf_op jit(solution)/shard_map/ppermute | solution.py:609
  172.6 14.8 %collective-permute-start.18 = (bf16[9,120,128]{2,1,0:T(8,128)(2,1)}, bf16[9,120,128]{2,1,0:T(8,128)(2,1)}, u32[]{:S(2)}, u32[]{:S(2)}) collective-permute-start(bf16[9,120,128]{2,1,0:T(8,128)(2,1)} %collective-permute-done.17), channel_id=1, source_target_pairs={{0,32},{16,48},{32,0},{48,16},{64,96},{80,112},{96,64},{112,80},{1... | collective-permute-start | bytes 829448 | tf_op jit(solution)/shard_map/ppermute | solution.py:609
  178.5 9.7 %collective-permute-start.21 = (bf16[9,120,128]{2,1,0:T(8,128)(2,1)}, bf16[9,120,128]{2,1,0:T(8,128)(2,1)}, u32[]{:S(2)}, u32[]{:S(2)}) collective-permute-start(bf16[9,120,128]{2,1,0:T(8,128)(2,1)} %collective-permute-done.20), channel_id=1, source_target_pairs={{0,16},{16,32},{32,48},{48,0},{64,80},{80,96},{96,112},{112,64},{1... | collective-permute-start | bytes 829448 | tf_op jit(solution)/shard_map/ppermute | solution.py:609
  (15 other events, 113.7 us)
